TPU v7x, 32 devices: a whole 2x2x4 slice. The times are simulated.
32 devices in a mesh: row: 2 (over y), col: 16 (over z, x, core).
Axes of the slice: x: 2, y: 2, z: 4, core: 2. Of those that a mesh axis runs over, the one named last changes fastest.
Arguments:
- ancestor_inv: float32 [16384, 16384], P('row', 'col'), may hold values from -0.0625 to 0.0625
- factor_rows: float32 [16384, 768], P(('row', 'col')), may hold values from -1.2 to 1.2
- diagonal_inv: float32 [3, 256, 256], replicated, may hold values from -6 to 6
- fill_list: int32 [3, 64], replicated, may hold values 0 or 1
Outputs:
- column_block: float32 [16384, 768], P(('row', 'col'))
- diagonal_block: float32 [3, 256, 256], replicated
All inputs are finite; a program needn't handle non-finite values.
Results may differ from a plain program's by a relative error of at most 0.000071.
Values sent between devices are 32-bit elements; how exact they have to be, the bound alone decides.
No kernel may reach another device: no remote copies, remote signals or barrier semaphores. Data moves between devices by JAX's collectives and lax.ppermute only.
A program may use at most 128 MiB of HBM per device.

v0:
```python
import jax
import jax.numpy as jnp
from jax import lax
from jax.sharding import PartitionSpec as P

W = 256
SIBS = 3
TILE = 256


def spread(block, axis, holder):
    block = jnp.where(lax.axis_index(axis) == holder, block, jnp.zeros_like(block))
    return lax.psum(block, axis)


def row_masks(fill_list, first_row, row_count):
    positions = first_row + jnp.arange(row_count, dtype=jnp.int32)
    tile_index = positions // TILE
    one_hot = (
        tile_index[:, None] == jnp.arange(fill_list.shape[1], dtype=jnp.int32)[None, :]
    ).astype(jnp.float32)
    return jnp.dot(one_hot, fill_list.T.astype(jnp.float32), precision=lax.Precision.HIGHEST)


def local(ancestor_inv, factor_rows, diagonal_inv, fill_list):
    row_devices = lax.axis_size("row")
    col_devices = lax.axis_size("col")
    group_span = col_devices // row_devices
    own_rows = factor_rows.shape[0]
    band_rows = ancestor_inv.shape[0]
    block_rows = ancestor_inv.shape[1]
    row_index = lax.axis_index("row")
    col_index = lax.axis_index("col")
    first_row = row_index * band_rows + col_index * own_rows
    local_mask = row_masks(fill_list, first_row, own_rows)
    wide_mask = jnp.repeat(local_mask, W, axis=1)
    masked = factor_rows * wide_mask
    band = lax.all_gather(masked, "col", axis=0, tiled=True)
    offset = col_index % group_span * block_rows
    section = lax.dynamic_slice_in_dim(band, offset, block_rows, 0)
    factor_block = spread(section, "row", col_index // group_span)
    summed = lax.psum_scatter(
        jnp.dot(ancestor_inv, factor_block, precision=lax.Precision.HIGHEST),
        "col",
        scatter_dimension=0,
        tiled=True,
    )
    column_block = -summed * wide_mask
    left_side = masked.reshape(own_rows, SIBS, W)
    right_side = column_block.reshape(own_rows, SIBS, W)
    local_term = jnp.einsum("rkw,rkv->kwv", left_side, right_side, precision=lax.Precision.HIGHEST)
    update = lax.psum(local_term, ("row", "col"))
    return (column_block, diagonal_inv - update)


def solution(mesh):
    placed = (P("row", "col"), P(("row", "col"), None), P(), P())
    return jax.shard_map(
        local, mesh=mesh, in_specs=placed, out_specs=(P(("row", "col"), None), P()), check_vma=False
    )
```

profile of v0, /device:TPU:0, one launch (start us, length us, event | category | flops | bytes accessed | tf_op | source)
XLA Modules:
  0.0 705.6 jit_solution(52910641871061557)
XLA Ops:
  7.2 0.0 all-gather.2.cloned.1.call-start
  7.2 0.0 copy-start.2
  7.2 1.9 copy.6
  9.1 0.0 copy-done.2
  9.1 0.3 fusion
  9.5 1.4 bitcast_multiply_fusion.1
  10.8 0.0 all-gather.2.cloned.1.call-update
  10.8 0.0 all-reduce.3.cloned.1.call-start
  10.9 131.3 %all-gather.2.cloned.1.call-done = f32[8192,768]{0,1:T(8,128)} async-done(((f32[512,768]{0,1:T(8,128)}), f32[8192,768]{0,1:T(8,128)}) %all-gather.2.cloned.1.call-update) | async-done | bytes 25165840 | tf_op jit(solution)/shard_map/all_gather | solution.py:38
  142.2 4.1 dynamic-slice_select_fusion
  146.3 0.0 all-reduce.3.cloned.1.call-update
  146.4 0.0 reduce-scatter.2.cloned.1.call-start
  146.4 85.9 %all-reduce.3.cloned.1.call-done = f32[1024,768]{0,1:T(8,128)} async-done(((f32[1024,768]{0,1:T(8,128)}), f32[1024,768]{0,1:T(8,128)}) %all-reduce.3.cloned.1.call-update) | async-done | bytes 3145744 | tf_op jit(solution)/shard_map/psum | solution.py:13
  232.3 86.1 %convolution_bitcast_fusion = f32[8192,768]{0,1:T(8,128)} fusion(f32[1024,768]{0,1:T(8,128)} %all-reduce.3.cloned.1.call-done, f32[8192,1024]{1,0:T(8,128)} %param.4), kind=kOutput, calls=%fused_computation | convolution fusion | flops 77309411328 | bytes 61865984 | tf_op jit(solution)/shard_map/dot_general | solution.py:43
  318.4 0.0 reduce-scatter.2.cloned.1.call-update
  318.4 0.0 copy-start
  318.4 0.0 all-reduce.5.cloned.1.call-start
  318.5 243.9 %reduce-scatter.2.cloned.1.call-done = f32[512,768]{0,1:T(8,128)} async-done(((f32[8192,768]{0,1:T(8,128)}), f32[512,768]{0,1:T(8,128)}) %reduce-scatter.2.cloned.1.call-update) | async-done | bytes 1572880 | tf_op jit(solution)/shard_map/reduce_scatter | solution.py:42
  562.3 1.6 bitcast_multiply_fusion
  563.9 0.0 copy-done
  563.9 2.5 fusion.6
  566.4 0.0 all-reduce.5.cloned.1.call-update
  566.5 0.0 copy-start.1
  566.5 1.6 copy.8
  568.1 128.8 %all-reduce.5.cloned.1.call-done = f32[3,256,256]{2,1,0:T(8,128)} async-done(((f32[3,256,256]{2,1,0:T(8,128)}), f32[3,256,256]{2,1,0:T(8,128)}) %all-reduce.5.cloned.1.call-update) | async-done | bytes 786448 | tf_op jit(solution)/shard_map/psum | solution.py:52
  696.9 0.0 copy-done.1
  696.9 2.2 sub.15
  (1 shorter events, 0.0 us)
Async XLA Ops:
  7.2 135.1 %all-gather.2.cloned.1.call-start = ((), (), s32[]{:S(2)}) async-start(), calls=%async_computation.1 | async-start | bytes 26738688 | tf_op jit(solution)/shard_map/all_gather | solution.py:38
  7.2 1.9 copy-start.2
  10.8 221.4 %all-reduce.3.cloned.1.call-start = ((), (), s32[]{:S(2)}) async-start(), calls=%async_computation.2 | async-start | bytes 6291456 | tf_op jit(solution)/shard_map/psum | solution.py:13
  146.4 416.0 %reduce-scatter.2.cloned.1.call-start = ((), (), s32[]{:S(2)}) async-start(), calls=%async_computation.3 | async-start | bytes 26738688 | tf_op jit(solution)/shard_map/reduce_scatter | solution.py:42
  318.4 245.5 %copy-start = (f32[512,768]{0,1:T(8,128)S(1)}, f32[512,768]{0,1:T(8,128)}, u32[]{:S(2)}) copy-start(f32[512,768]{0,1:T(8,128)} %bitcast_multiply_fusion.1) | copy-start | bytes 4718596
  318.4 378.5 %all-reduce.5.cloned.1.call-start = ((), (), s32[]{:S(2)}) async-start(), calls=%async_computation.4 | async-start | bytes 1572864 | tf_op jit(solution)/shard_map/psum | solution.py:52
  566.5 130.4 %copy-start.1 = (f32[3,256,256]{2,1,0:T(8,128)S(1)}, f32[3,256,256]{2,1,0:T(8,128)}, u32[]{:S(2)}) copy-start(f32[3,256,256]{2,1,0:T(8,128)} %param.6) | copy-start | bytes 2359300
Sparse Core Ops, SparseCore 0:
  11.0 131.2 all-gather.1
  146.5 85.7 all-reduce.2
  318.5 243.7 reduce-scatter.1
  568.8 128.0 all-reduce.4
where the time goes:
time: 706 us
  waiting for transfers between devices  590 us (84%)
  matrix products  88.9 us (13%)
  between operations  13.9 us (2%)
  other arithmetic  9.27 us (1%)
    reduce_scatter x1, waiting for transfers between devices, local(): lax.psum_scatter(jnp.dot(ancestor_inv, factor_block, precision=lax.Precis...  244 us
    all_gather x1, waiting for transfers between devices, local(): band = lax.all_gather(masked, 'col', axis=0, tiled=True)  131 us
    psum x1, waiting for transfers between devices, local(): update = lax.psum(local_term, ('row', 'col'))  129 us
    dot_general x1, matrix products, local(): jnp.dot(ancestor_inv, factor_block, precision=lax.Precision.HIGHEST)  86.1 us
    psum x1, waiting for transfers between devices, spread(): return lax.psum(block, axis)  85.9 us
  transfers between devices with their start and end apart: 4, of which 4 were waited for; matrix products, arithmetic and copies ran while one was open for 0% of the time, Pallas kernels for 0%

commit v1 on v0

v1 whole, which is shorter than its diff:
```python
import functools

import jax
import jax.numpy as jnp
import numpy as np
from jax import lax
from jax.experimental import pallas as pl
from jax.experimental.pallas import tpu as pltpu
from jax.sharding import PartitionSpec as P

W = 256
SIBS = 3
TILE = 256
LANES = 128
CHUNKS = W // LANES
VMEM_LIMIT = 32 * 1024 * 1024
MULTIPLY_VMEM = 24 * 1024 * 1024
STRIPS = (((0, 2, 0), (2, 4, 1)), ((0, 2, 0), (2, 4, 1)))
SLOTS = 6
LONG = pl.CostEstimate(flops=10**11, bytes_accessed=1, transcendentals=0)
TOKEN = jax.ShapeDtypeStruct((1,), jnp.int32)
SMEM = pltpu.SMEM
VMEM = pltpu.VMEM


class Plan:
    def __init__(self, row_devices, col_devices, own_rows, band_rows, block_rows):
        self.row_devices, self.col_devices = row_devices, col_devices
        self.own_rows, self.band_rows, self.block_rows = own_rows, band_rows, block_rows
        self.bits = col_devices.bit_length() - 1
        self.high = min(TILE, own_rows)
        self.half = self.high // 2
        self.sub = TILE // self.high
        self.per = own_rows // self.high
        self.tile_rows = band_rows // self.high
        self.blocks = band_rows // TILE
        self.tiles = self.tile_rows * SIBS
        first = list(range(1, self.bits))
        second = [2, 1] + first[2:] if self.bits > 2 else first
        self.steps = len(first)
        self.orders = (first, second)
        unit = self.half // 4
        self.strips = [[(a * unit, b * unit, order) for a, b, order in chunk] for chunk in STRIPS]

    def sequence(self, order, step):
        same = self.orders[0] == self.orders[1] or step > 1
        return (0 if same else order) * self.steps + step

    def pos_row(self, order, step):
        return 3 * self.sequence(order, step)

    def give_row(self, order, step):
        return 1 + self.pos_row(order, step)

    def hold_row(self, order, step):
        return 2 + self.pos_row(order, step)

    def block_row(self, k):
        return 6 * self.steps + k

    @property
    def count_row(self):
        return 6 * self.steps + SIBS

    def give_count(self, order, step):
        return 2 * self.sequence(order, step)

    def hold_count(self, order, step):
        return 1 + self.give_count(order, step)

    def block_count(self, k):
        return 4 * self.steps + k


def plan_kernel(plan, where_ref, fill_ref, table_ref):
    row_index, col_index = where_ref[0], where_ref[1]
    every = [(order, step) for order in range(2) for step in range(plan.steps)]
    sequences = list({plan.sequence(*each): each for each in every}.values())
    zero = jnp.int32(0)

    def one_block(block, counts):
        result = []
        for k in range(SIBS):
            table_ref[plan.block_row(k), counts[k]] = block
            result.append(counts[k] + fill_ref[k, row_index * plan.blocks + block])
        return tuple(result)

    counts = lax.fori_loop(0, plan.blocks, one_block, (zero,) * SIBS)
    for k in range(SIBS):
        table_ref[plan.count_row, plan.block_count(k)] = counts[k]

    def one_tile(tile, counts):
        tile_row, sibling = tile // SIBS, tile % SIBS
        apart = (tile_row // plan.per) ^ col_index

        def place(counts):
            result = []
            for number, (order, step) in enumerate(sequences):
                held, sent = counts[2 * number], counts[2 * number + 1]
                bits = plan.orders[order]
                earlier = sum(1 << bit for bit in bits[:step])
                here = 1 << bits[step]
                table_ref[plan.pos_row(order, step), tile] = held
                table_ref[plan.hold_row(order, step), held] = tile
                table_ref[plan.give_row(order, step), sent] = tile
                keeps = (apart & (earlier | here)) == 0
                gives = (apart & (earlier | here)) == here
                result += [held + keeps.astype(jnp.int32), sent + gives.astype(jnp.int32)]
            return tuple(result)

        active = fill_ref[sibling, (row_index * plan.tile_rows + tile_row) // plan.sub] != 0
        return lax.cond(active, place, lambda counts: counts, counts)

    counts = lax.fori_loop(0, plan.tiles, one_tile, (zero,) * (2 * len(sequences)))
    for number, (order, step) in enumerate(sequences):
        table_ref[plan.count_row, plan.hold_count(order, step)] = counts[2 * number]
        table_ref[plan.count_row, plan.give_count(order, step)] = counts[2 * number + 1]


def make_plan(plan, where, fill_list):
    width = -(-(plan.tiles + 1) // 128) * 128
    return pl.pallas_call(
        functools.partial(plan_kernel, plan),
        out_shape=jax.ShapeDtypeStruct((plan.count_row + 1, width), jnp.int32),
        in_specs=[pl.BlockSpec(memory_space=SMEM)] * 2,
        out_specs=pl.BlockSpec(memory_space=SMEM),
        name="plan",
    )(where, fill_list)


def split_high_low(values):
    high = values.astype(jnp.bfloat16)
    return high, (values - high.astype(jnp.float32)).astype(jnp.bfloat16)


def multiply_kernel(plan, k, column, where_ref, fill_ref, table_ref, token_ref, inverse_ref, *refs):
    pieces = refs[: plan.row_devices]
    keep_ref, send_ref, done_ref, factor_ref, rows_ref, high_ref, low_ref, total_ref, sems = refs[plan.row_devices :]
    done_ref[0] = token_ref[0]
    row_index, col_index = where_ref[0], where_ref[1]
    core = col_index % 2
    count = table_ref[plan.count_row, plan.block_count(k)]

    def fetch(number, slot):
        start = pl.multiple_of(table_ref[plan.block_row(k), number] * TILE, TILE)
        return pltpu.make_async_copy(inverse_ref.at[pl.ds(start, TILE), :], rows_ref.at[slot], sems.at[slot])

    for ahead in range(SLOTS - 1):

        @pl.when(ahead < count)
        def _(ahead=ahead):
            fetch(ahead, ahead).start()

    for shift in range(plan.row_devices):
        source = lax.rem(row_index - shift + plan.row_devices, plan.row_devices)
        for part in range(plan.per):
            start = pl.multiple_of(source * plan.own_rows + part * plan.high, plan.high)
            filled = fill_ref[k, (col_index * plan.block_rows + start) // TILE].astype(jnp.float32)
            piece = pieces[shift][part * plan.high : (part + 1) * plan.high, column : column + LANES]
            high, low = split_high_low(piece * filled)
            factor_ref[pl.ds(start, plan.high), :LANES] = high
            factor_ref[pl.ds(start, plan.high), LANES:] = low

    def one(number, carry):
        slot = lax.rem(number, SLOTS)
        fetch(number, slot).wait()

        @pl.when(number + SLOTS - 1 < count)
        def _():
            fetch(number + SLOTS - 1, lax.rem(number + SLOTS - 1, SLOTS)).start()

        high, low = split_high_low(rows_ref[slot])
        high_ref[...] = high
        low_ref[...] = low
        wide = jnp.dot(high_ref[...], factor_ref[...], preferred_element_type=jnp.float32)
        narrow = jnp.dot(low_ref[...], factor_ref[:, :LANES], preferred_element_type=jnp.float32)
        total_ref[...] = wide[:, :LANES] + (wide[:, LANES:] + narrow)
        first = table_ref[plan.block_row(k), number] * plan.sub
        for part in range(plan.sub):
            near = pl.multiple_of(part * plan.high + core * plan.half, plan.half)
            far = pl.multiple_of(part * plan.high + (1 - core) * plan.half, plan.half)
            keep_ref[first + part] = total_ref[pl.ds(near, plan.half), :]
            send_ref[first + part] = total_ref[pl.ds(far, plan.half), :]
        return carry

    lax.fori_loop(0, count, one, 0)


def multiply(plan, k, column, where, fill_list, table, token, inverse, pieces):
    shape = jax.ShapeDtypeStruct((plan.tile_rows, plan.half, LANES), jnp.float32)
    smem, vmem = pl.BlockSpec(memory_space=SMEM), pl.BlockSpec(memory_space=VMEM)
    return pl.pallas_call(
        functools.partial(multiply_kernel, plan, k, column),
        out_shape=(shape, shape, TOKEN),
        in_specs=[smem, smem, smem, smem, pl.BlockSpec(memory_space=pl.ANY)] + [vmem] * len(pieces),
        out_specs=(vmem, vmem, smem),
        scratch_shapes=[
            VMEM((plan.block_rows, 2 * LANES), jnp.bfloat16),
            VMEM((SLOTS, TILE, plan.block_rows), jnp.float32),
            VMEM((TILE, plan.block_rows), jnp.bfloat16),
            VMEM((TILE, plan.block_rows), jnp.bfloat16),
            VMEM((TILE, LANES), jnp.float32),
            pltpu.SemaphoreType.DMA((SLOTS,)),
        ],
        compiler_params=pltpu.CompilerParams(vmem_limit_bytes=MULTIPLY_VMEM),
        cost_estimate=LONG,
        name="multiply",
    )(where, fill_list, table, token, inverse, *pieces)


def call_local(kernel, out_shape, tables, token, operands, name, scratch=(), ahead=()):
    vmem, smem = pl.BlockSpec(memory_space=VMEM), pl.BlockSpec(memory_space=SMEM)

    def body(*refs):
        tables_in, token_ref, rest = refs[: len(tables)], refs[len(tables)], refs[len(tables) + len(ahead) + 1 :]
        last = len(operands) + len(out_shape)
        rest[last][0] = token_ref[0]
        kernel(*tables_in, *rest[:last], *rest[last + 1 :])

    return pl.pallas_call(
        body,
        out_shape=tuple(out_shape) + (TOKEN,),
        in_specs=[smem] * (len(tables) + 1) + [pl.BlockSpec(memory_space=pl.ANY)] * len(ahead) + [vmem] * len(operands),
        out_specs=(vmem,) * len(out_shape) + (smem,),
        scratch_shapes=scratch,
        compiler_params=pltpu.CompilerParams(vmem_limit_bytes=VMEM_LIMIT),
        cost_estimate=LONG,
        name=name,
    )(*tables, token, *ahead, *operands)


def tile_lists(plan, table_ref, step, order, outs):
    yield outs[0], plan.give_row(order, step), table_ref[plan.count_row, plan.give_count(order, step)]
    yield outs[1], plan.hold_row(order, step), table_ref[plan.count_row, plan.hold_count(order, step)]


def relay_kernel(in_ref, out_ref):
    out_ref[...] = in_ref[...]


def later_kernel(in_ref, out_ref):
    for k in range(SIBS):
        start = k * W + LANES
        out_ref[:, k * LANES : (k + 1) * LANES] = in_ref[:, start : start + LANES]


def merge_kernel(plan, strips, table_ref, *refs):
    keep, core, outs = refs[:SIBS], refs[SIBS : 2 * SIBS], refs[2 * SIBS :]
    for number, (first, last, order) in enumerate(strips):
        for out_ref, row, count in tile_lists(plan, table_ref, 0, order, outs[2 * number : 2 * number + 2]):

            def one(slot, carry, out_ref=out_ref, row=row, first=first, last=last):
                tile = table_ref[row, slot]
                tile_row, sibling = tile // SIBS, tile % SIBS
                for k in range(SIBS):

                    @pl.when(sibling == k)
                    def _(k=k):
                        out_ref[slot] = keep[k][tile_row, first:last, :] + core[k][tile_row, first:last, :]

                return carry

            lax.fori_loop(0, count, one, 0)


def step_kernel(plan, strips, step, table_ref, *refs):
    size = len(strips)
    for number, (_, _, order) in enumerate(strips):
        held_ref, came_ref = refs[number], refs[size + number]
        outs = refs[2 * size + 2 * number : 2 * size + 2 * number + 2]
        for out_ref, row, count in tile_lists(plan, table_ref, step, order, outs):

            def one(slot, carry, out_ref=out_ref, row=row, order=order, held_ref=held_ref, came_ref=came_ref):
                place = table_ref[plan.pos_row(order, step - 1), table_ref[row, slot]]
                out_ref[slot] = held_ref[place] + came_ref[place]
                return carry

            lax.fori_loop(0, count, one, 0)


def strip_shapes(cap, strip):
    return (jax.ShapeDtypeStruct((cap, strip[1] - strip[0], LANES), jnp.float32),) * 2


def collect_kernel(plan, strips, where_ref, fill_ref, table_ref, *refs):
    size = len(strips)
    held, came, (near_ref, far_ref) = refs[:size], refs[size : 2 * size], refs[2 * size :]
    row_index, col_index = where_ref[0], where_ref[1]
    for out_ref, owner in ((near_ref, col_index), (far_ref, col_index ^ 1)):
        for part in range(plan.per):
            for k in range(SIBS):
                tile_row = owner * plan.per + part
                tile = tile_row * SIBS + k
                active = fill_ref[k, (row_index * plan.tile_rows + tile_row) // plan.sub] != 0
                place = part * SIBS + k

                @pl.when(active)
                def _(out_ref=out_ref, tile=tile, place=place):
                    for number, (first, last, order) in enumerate(strips):
                        source = table_ref[plan.pos_row(order, plan.steps - 1), tile]
                        out_ref[place, first:last, :] = -(held[number][source] + came[number][source])

                @pl.when(jnp.logical_not(active))
                def _(out_ref=out_ref, place=place):
                    out_ref[place] = jnp.zeros(out_ref.shape[1:], jnp.float32)


def finish_kernel(plan, where_ref, factor_ref, *refs):
    parts, (block_ref, term_ref) = refs[: 2 * CHUNKS], refs[2 * CHUNKS :]
    core = where_ref[1] % 2
    for chunk in range(CHUNKS):
        near_ref, far_ref = parts[2 * chunk], parts[2 * chunk + 1]
        for part in range(plan.per):
            near = pl.multiple_of(part * plan.high + core * plan.half, plan.half)
            far = pl.multiple_of(part * plan.high + (1 - core) * plan.half, plan.half)
            for k in range(SIBS):
                columns = slice(k * W + chunk * LANES, k * W + (chunk + 1) * LANES)
                block_ref[pl.ds(near, plan.half), columns] = near_ref[part * SIBS + k]
                block_ref[pl.ds(far, plan.half), columns] = far_ref[part * SIBS + k]
    for k in range(SIBS):
        columns = slice(k * W, (k + 1) * W)
        term_ref[columns, :] = lax.dot_general(
            factor_ref[:, columns],
            block_ref[:, columns],
            (((0,), (0,)), ((), ())),
            precision=lax.Precision.HIGHEST,
            preferred_element_type=jnp.float32,
        )


def toggled(value, mask, devices):
    return lax.ppermute(value, ("row", "col"), [(i, i ^ mask) for i in range(devices)])


def sum_everywhere(plan, value):
    cols, devices = plan.col_devices, plan.row_devices * plan.col_devices
    me = lax.axis_index("row") * cols + lax.axis_index("col")
    masks = [1 << bit for bit in range(devices.bit_length() - 1)]
    row_masks = [m for m in masks if m >= cols]
    col_masks = [m for m in masks if m < cols]
    rest = col_masks[2:] + row_masks[1:]
    groups = [col_masks[:1], col_masks[1:2] + row_masks[:1]]
    groups += [rest[i : i + 2] for i in range(0, len(rest), 2)]

    def member(group):
        return sum(((me & mask) != 0).astype(jnp.int32) << n for n, mask in enumerate(group))

    def spread(group, number):
        return sum(mask for n, mask in enumerate(group) if number >> n & 1)

    for group in groups[:-1]:
        size = 1 << len(group)
        rows = value.shape[0] // size
        mine = member(group)
        sent = [
            toggled(lax.dynamic_slice_in_dim(value, (mine ^ d) * rows, rows, 0), spread(group, d), devices)
            for d in range(1, size)
        ]
        own = lax.dynamic_slice_in_dim(value, mine * rows, rows, 0)
        value = functools.reduce(jnp.add, sent, own)
    group = groups[-1]
    arrived = [toggled(value, spread(group, d), devices) for d in range(1, 1 << len(group))]
    mine = member(group)
    whole = jnp.stack([value] + arrived)
    ordered = [lax.dynamic_index_in_dim(whole, mine ^ n, 0, False) for n in range(1 << len(group))]
    value = functools.reduce(jnp.add, ordered)
    for group in reversed(groups[:-1]):
        size = 1 << len(group)
        mine = member(group)
        parts = [value] + [toggled(value, spread(group, d), devices) for d in range(1, size)]
        whole = jnp.stack(parts)
        value = jnp.concatenate([lax.dynamic_index_in_dim(whole, mine ^ n, 0, False) for n in range(size)])
    return value


def cross(plan, value):
    rows, cols = plan.row_devices, plan.col_devices
    if rows != 2:
        return value
    pairs = [(r * cols + c, (c & 1) * cols + (c & ~1 | r)) for r in range(rows) for c in range(cols)]
    return lax.ppermute(value, ("row", "col"), pairs)


def home(plan, value):
    rows, cols = plan.row_devices, plan.col_devices
    if rows != 2:
        pairs = [(rows * j + h, h * cols + j) for j in range(cols) for h in range(rows)]
    else:
        pairs = []
        for y in range(rows):
            for c in range(cols):
                pairs.append((y * cols + c, y * cols + ((c & 1) * cols + (c & ~1 | y)) // 2))
    return lax.ppermute(value, ("row", "col"), pairs)


def sparse(plan, caps, ancestor_inv, factor_rows, diagonal_inv, fill_list):
    rows, cols = plan.row_devices, plan.col_devices
    where = jnp.stack([lax.axis_index("row"), lax.axis_index("col")]).astype(jnp.int32)
    table = make_plan(plan, where, fill_list)
    pair = [(i, i ^ 1) for i in range(cols)]
    token = jnp.zeros(TOKEN.shape, TOKEN.dtype)
    tile_set = jax.ShapeDtypeStruct((plan.per * SIBS, plan.half, LANES), jnp.float32)

    def over_rows(own):
        turns = [[(i, (i + shift) % rows) for i in range(rows)] for shift in range(1, rows)]
        return [own] + [lax.ppermute(own, "row", turn) for turn in turns]

    def product(k, column, pieces, token):
        near, far, token = multiply(plan, k, column, where, fill_list, table, token, ancestor_inv, pieces)
        return [near, lax.ppermute(far, "col", pair)], token

    def relay(value, token):
        shape = jax.ShapeDtypeStruct(value.shape, value.dtype)
        return call_local(relay_kernel, (shape,), [], token, [value], "relay")

    def later_columns(token):
        shape = jax.ShapeDtypeStruct((factor_rows.shape[0], SIBS * LANES), jnp.float32)
        return call_local(later_kernel, (shape,), [], token, [factor_rows], "later_columns")

    def exchange(chunk, step, made):
        strips = plan.strips[chunk]
        held, came = [], []
        for number, strip in enumerate(strips):
            bit = 1 << plan.orders[strip[2]][step]
            came.append(lax.ppermute(made[2 * number], "col", [(i, i ^ bit) for i in range(cols)]))
            held.append(made[2 * number + 1])
        return held + came

    def merge(chunk, operands, token):
        strips = plan.strips[chunk]
        shapes = sum((strip_shapes(caps[1], strip) for strip in strips), ())
        *made, token = call_local(functools.partial(merge_kernel, plan, strips), shapes, [table], token, operands, "merge")
        return exchange(chunk, 0, made), token

    def step(chunk, number, operands, token):
        strips = plan.strips[chunk]
        shapes = sum((strip_shapes(caps[number + 1], strip) for strip in strips), ())
        kernel = functools.partial(step_kernel, plan, strips, number)
        *made, token = call_local(kernel, shapes, [table], token, operands, "step")
        return exchange(chunk, number, made), token

    def collect(chunk, operands, token):
        kernel = functools.partial(collect_kernel, plan, plan.strips[chunk])
        tables = [where, fill_list, table]
        near, far, token = call_local(kernel, (tile_set, tile_set), tables, token, operands, "collect")
        return [near, lax.ppermute(far, "col", pair)], token

    def finish(parts, token):
        shapes = (
            jax.ShapeDtypeStruct(factor_rows.shape, jnp.float32),
            jax.ShapeDtypeStruct((SIBS * W, W), jnp.float32),
        )
        kernel = functools.partial(finish_kernel, plan)
        return call_local(kernel, shapes, [where], token, [factor_rows] + parts, "finish")

    def sums(made):
        return [near for near, _ in made] + [core for _, core in made]

    pieces = []
    for k in range(SIBS):
        columns = factor_rows[:, k * W : k * W + LANES]
        pieces.append(over_rows(home(plan, cross(plan, columns))))
    made = [None] * SIBS
    made[0], token = product(0, 0, pieces[0], token)
    columns, token = later_columns(token)
    made[1], token = product(1, 0, pieces[1], token)
    columns, token = relay(cross(plan, columns), token)
    made[2], token = product(2, 0, pieces[2], token)
    first, token = merge(0, sums(made), token)
    columns, token = relay(home(plan, columns), token)
    later = over_rows(columns)
    first, token = step(0, 1, first, token)
    made[0], token = product(0, 0, later, token)
    made[1], token = product(1, LANES, later, token)
    first, token = step(0, 2, first, token)
    made[2], token = product(2, 2 * LANES, later, token)
    second, token = merge(1, sums(made), token)
    for number in range(3, plan.steps):
        first, token = step(0, number, first, token)
        second, token = step(1, number - 2, second, token)
    first, token = collect(0, first, token)
    second, token = step(1, plan.steps - 2, second, token)
    second, token = step(1, plan.steps - 1, second, token)
    second, token = collect(1, second, token)
    column_block, term, token = finish(first + second, token)
    update = sum_everywhere(plan, term).reshape(diagonal_inv.shape)
    return column_block, diagonal_inv - update


def row_masks(fill_list, first_row, row_count):
    positions = first_row + jnp.arange(row_count, dtype=jnp.int32)
    tile_index = positions // TILE
    one_hot = (
        tile_index[:, None] == jnp.arange(fill_list.shape[1], dtype=jnp.int32)[None, :]
    ).astype(jnp.float32)
    return jnp.dot(one_hot, fill_list.T.astype(jnp.float32), precision=lax.Precision.HIGHEST)


def dense(ancestor_inv, factor_rows, diagonal_inv, fill_list):
    row_devices, col_devices = lax.axis_size("row"), lax.axis_size("col")
    group_span = col_devices // row_devices
    own_rows = factor_rows.shape[0]
    band_rows, block_rows = ancestor_inv.shape
    row_index, col_index = lax.axis_index("row"), lax.axis_index("col")
    first_row = row_index * band_rows + col_index * own_rows
    wide_mask = jnp.repeat(row_masks(fill_list, first_row, own_rows), W, axis=1)
    masked = factor_rows * wide_mask
    band = lax.all_gather(masked, "col", axis=0, tiled=True)
    section = lax.dynamic_slice_in_dim(band, col_index % group_span * block_rows, block_rows, 0)
    section = jnp.where(row_index == col_index // group_span, section, jnp.zeros_like(section))
    product = jnp.dot(ancestor_inv, lax.psum(section, "row"), precision=lax.Precision.HIGHEST)
    summed = lax.psum_scatter(product, "col", scatter_dimension=0, tiled=True)
    column_block = -summed * wide_mask
    left_side = masked.reshape(own_rows, SIBS, W)
    right_side = column_block.reshape(own_rows, SIBS, W)
    local_term = jnp.einsum("rkw,rkv->kwv", left_side, right_side, precision=lax.Precision.HIGHEST)
    update = lax.psum(local_term, ("row", "col"))
    return column_block, diagonal_inv - update


def fill_groups(plan):
    devices = np.arange(plan.row_devices * plan.col_devices)
    columns, levels = [], []
    for order in plan.orders:
        for step in range(plan.steps + 1):
            mask = sum(1 << bit for bit in order[:step])
            key = (devices // plan.col_devices) * plan.col_devices + (devices % plan.col_devices & mask)
            for value in np.unique(key):
                columns.append(key == value)
                levels.append(step)
    member = np.stack(columns, axis=1).astype(np.float32)
    return np.repeat(member, plan.per, axis=0), np.array(levels)


SHARES = (((96, 96), (30, 48), (17, 24), (10, 12), (6, 6)), ((96, 96), (37, 48), (21, 24), (12, 12), (6, 6)))


def local(ancestor_inv, factor_rows, diagonal_inv, fill_list):
    plan = Plan(
        lax.axis_size("row"), lax.axis_size("col"), factor_rows.shape[0], ancestor_inv.shape[0], ancestor_inv.shape[1]
    )
    member, levels = fill_groups(plan)
    block_of = np.arange(member.shape[0]) // plan.sub
    spread = np.zeros((fill_list.shape[1], member.shape[1]), np.float32)
    np.add.at(spread, block_of, member)
    per_block = jnp.sum(fill_list, axis=0).astype(jnp.float32)
    found = jnp.sum(per_block[:, None] * spread, axis=0)
    limits, branches = [], []
    for shares in SHARES:
        caps = []
        for level in range(plan.steps + 1):
            size = plan.tiles >> level
            part, full = shares[min(level, len(shares) - 1)]
            caps.append(min(size, -(-size * part // full)))
        limits.append([caps[level] for level in levels])
        branches.append(functools.partial(sparse, plan, caps))
    branches.append(dense)
    index = jnp.sum(jnp.any(found[None, :] > np.array(limits, np.float32), axis=1).astype(jnp.int32))
    return lax.switch(index, branches, ancestor_inv, factor_rows, diagonal_inv, fill_list)


def solution(mesh):
    placed = (P("row", "col"), P(("row", "col"), None), P(), P())
    return jax.shard_map(
        local, mesh=mesh, in_specs=placed, out_specs=(P(("row", "col"), None), P()), check_vma=False
    )
```

time: 706 us -> 324 us (0.46)
  waiting for transfers between devices: 590 us -> 120 us
  Pallas kernels: 0 us -> 114 us
  matrix products: 88.9 us -> 0 us
  starting transfers between devices: 0.16 us -> 65.4 us
    reduce_scatter x1 -> x0, waiting for transfers between devices: 244 us -> none  [local(): lax.psum_scatter(jnp.dot(ancestor_inv, factor_block, precision=lax.Precis...]
    psum x2 -> x0, waiting for transfers between devices: 215 us -> none  [the longest x1 129 us: local(): update = lax.psum(local_term, ('row', 'col'))]
    all_gather x1 -> x0, waiting for transfers between devices: 131 us -> none  [local(): band = lax.all_gather(masked, 'col', axis=0, tiled=True)]
    ppermute x0 -> x43, waiting for transfers between devices: none -> 120 us  [the longest x12 95.9 us: exchange(): lax.ppermute(made[2 * number], 'col', [(i, i ^ bit) for i in range(cols)])]
    pallas_call x0 -> x19, Pallas kernels: none -> 114 us  [the longest x6 69.7 us: multiply(): pl.pallas_call(functools.partial(multiply_kernel, plan, k, column), out_s...]
    dot_general x3 -> x0, matrix products: 88.9 us -> none  [the longest x1 86.1 us: local(): jnp.dot(ancestor_inv, factor_block, precision=lax.Precision.HIGHEST)]
    ppermute x0 -> x43, starting transfers between devices: none -> 65.4 us  [the longest x12 27 us: exchange(): lax.ppermute(made[2 * number], 'col', [(i, i ^ bit) for i in range(cols)])]
  transfers between devices with their start and end apart: 4 -> 43, of which waited for: 4 -> 23; matrix products, arithmetic and copies ran while one was open for 0% -> 0% of each run, Pallas kernels for 0% -> 32%
where the time goes in v1:
time: 324 us; the launch traced here: 325 us
  waiting for transfers between devices  120 us (37%)
  Pallas kernels  114 us (35%)
  starting transfers between devices  65.4 us (20%)
  between operations  14.7 us (5%)
  other arithmetic  7.32 us (2%)
    ppermute x12, waiting for transfers between devices, exchange(): lax.ppermute(made[2 * number], 'col', [(i, i ^ bit) for i in range(cols)])  95.9 us
    pallas_call x6, Pallas kernels, multiply(): pl.pallas_call(functools.partial(multiply_kernel, plan, k, column), out_s...  69.7 us
    pallas_call x12, Pallas kernels, call_local(): pl.pallas_call(body, out_shape=tuple(out_shape) + (TOKEN,), in_specs=[sme...  37 us
    ppermute x12, starting transfers between devices, exchange(): lax.ppermute(made[2 * number], 'col', [(i, i ^ bit) for i in range(cols)])  27 us
    ppermute x11, waiting for transfers between devices, toggled(): lax.ppermute(value, ('row', 'col'), [(i, i ^ mask) for i in range(devices)])  18.1 us
    ppermute x4, starting transfers between devices, over_rows(): return [own] + [lax.ppermute(own, 'row', turn) for turn in turns]  14.3 us
    ppermute x11, starting transfers between devices, toggled(): lax.ppermute(value, ('row', 'col'), [(i, i ^ mask) for i in range(devices)])  11.8 us
    pallas_call x1, Pallas kernels, make_plan(): pl.pallas_call(functools.partial(plan_kernel, plan), out_shape=jax.ShapeD...  7.59 us
  transfers between devices with their start and end apart: 43, of which 23 were waited for; matrix products, arithmetic and copies ran while one was open for 0% of the time, Pallas kernels for 32%

profile of v1, /device:TPU:0, one launch (start us, length us, event | category | flops | bytes accessed | tf_op | source)
XLA Modules:
  0.0 324.7 jit_solution(991865617028332039)
XLA Ops:
  10.8 304.7 %conditional.1 = (f32[512,768]{1,0:T(8,128)}, f32[3,256,256]{2,1,0:T(8,128)}, f32[3,256,256]{2,1,0:T(8,128)}) conditional(s32[]{:T(128)} %clamp.3, (s32[3,64]{1,0:T(4,128)}, f32[512,768]{1,0:T(8,128)}, f32[8192,1024]{1,0:T(8,128)}, f32[3,256,256]{2,1,0:T(8,128)}) %tuple.19, (s32[3,64]{1,0:T(4,128)}, f32[512,768]{1,0:T(8,128)}, ...), branch_computations={%region_4.5_spmd, %region_5.6_spmd, %region_6.10_spmd} | conditional | flops 1800001290240 | bytes 275016032 | solution.py:559
  17.5 12.1 %collective-permute-start.2 = (f32[512,128]{1,0:T(8,128)S(1)}, f32[512,128]{1,0:T(8,128)S(1)}, u32[]{:S(2)}, u32[]{:S(2)}) collective-permute-start(f32[512,128]{1,0:T(8,128)S(1)} %collective-permute-done.1.refs_0_), channel_id=1, source_target_pairs={{0,16},{16,0},{1,17},{17,1},{2,18},{18,2},{3,19},{19,3},{4,20},{20... | collective-permute-start | bytes 786440 | tf_op jit(solution)/shard_map/cond/branch_0_fun/ppermute | solution.py:406
  30.3 7.6 %plan.2.table_ref.refs_0_.refs_2_ = s32[22,128]{1,0:T(8,128)} custom-call(s32[2]{0:T(128)} %pad_add_fusion.where_ref.refs_0_, s32[3,64]{1,0:T(4,128)} %get-tuple-element.24.fill_ref.refs_1_), custom_call_target="tpu_custom_call" | custom-call | tf_op jit(solution)/shard_map/cond/branch_0_fun/plan/pallas_call | solution.py:122
  38.0 2.0 collective-permute-start.5
  41.4 11.4 %multiply.12 = (f32[32,128,128]{2,1,0:T(8,128)S(1)}, f32[32,128,128]{2,1,0:T(8,128)}, s32[1]{0:T(128)}) custom-call(s32[2]{0:T(128)S(1)} %copy-done.4, s32[3,64]{1,0:T(4,128)} %get-tuple-element.24.fill_ref.refs_1_, s32[22,128]{1,0:T(8,128)S(1)} %copy-done, s32[1]{0:T(128)} %constant.131.clone.token_ref, f32[8192,1024]{1,0:T(8,128)} %get-tuple-element.25.inverse_ref, ...), custom_call_target="tpu_custom_call" | custom-call | flops 99999997952 | bytes 1 | tf_op jit(solution)/shard_map/cond/branch_0_fun/multiply/pallas_call | solution.py:192
  54.7 3.9 %collective-permute-start.10 = (f32[32,128,128]{2,1,0:T(8,128)}, f32[32,128,128]{2,1,0:T(8,128)}, u32[]{:S(2)}, u32[]{:S(2)}) collective-permute-start(f32[32,128,128]{2,1,0:T(8,128)} %get-tuple-element.36), channel_id=1, source_target_pairs={{0,1},{1,0},{2,3},{3,2},{4,5},{5,4},{6,7},{7,6},{8,9},{9,8},{10,11... | collective-permute-start | bytes 6291464 | tf_op jit(solution)/shard_map/cond/branch_0_fun/ppermute | solution.py:410
  58.6 12.2 %multiply.13 = (f32[32,128,128]{2,1,0:T(8,128)S(1)}, f32[32,128,128]{2,1,0:T(8,128)}, s32[1]{0:T(128)}) custom-call(s32[2]{0:T(128)S(1)} %copy-done.5, s32[3,64]{1,0:T(4,128)S(1)} %copy-done.15, s32[22,128]{1,0:T(8,128)S(1)} %copy-done.1, s32[1]{0:T(128)} %get-tuple-element.28.token_ref, f32[8192,1024]{1,0:T(8,128)} %get-tuple-element.25.inverse_ref, ...), custom_call_target="tpu_custom_call" | custom-call | flops 99999997952 | bytes 1 | tf_op jit(solution)/shard_map/cond/branch_0_fun/multiply/pallas_call | solution.py:192
  72.2 11.4 %multiply.14 = (f32[32,128,128]{2,1,0:T(8,128)S(1)}, f32[32,128,128]{2,1,0:T(8,128)S(1)}, s32[1]{0:T(128)}) custom-call(s32[2]{0:T(128)S(1)} %copy-done.5, s32[3,64]{1,0:T(4,128)S(1)} %copy-done.15, s32[22,128]{1,0:T(8,128)S(1)} %copy-done.1, s32[1]{0:T(128)} %get-tuple-element.31.token_ref, f32[8192,1024]{1,0:T(8,128)} %get-tuple-element.25.inverse_ref, ...), custom_call_target="tpu_custom_call" | custom-call | flops 99999997952 | bytes 1 | tf_op jit(solution)/shard_map/cond/branch_0_fun/multiply/pallas_call | solution.py:192
  84.8 3.1 collective-permute-done.12.refs_7_
  87.8 7.2 %merge.4 = (f32[30,64,128]{2,1,0:T(8,128)S(1)}, f32[30,64,128]{2,1,0:T(8,128)S(1)}, f32[30,64,128]{2,1,0:T(8,128)S(1)}, f32[30,64,128]{2,1,0:T(8,128)S(1)}, s32[1]{0:T(128)}) custom-call(s32[22,128]{1,0:T(8,128)S(1)} %copy-done.1, s32[1]{0:T(128)} %get-tuple-element.32.refs_1_, f32[32,128,128]{2,1,0:T(8,128)S(1)} %get-tuple-element.33.refs_2_, ...), custom_call_target="tpu_custom_call" | custom-call | flops 99999997952 | bytes 1 | tf_op jit(solution)/shard_map/cond/branch_0_fun/merge/pallas_call | solution.py:220
  95.1 2.3 collective-permute-start.14
  97.4 6.4 %collective-permute-start.15 = (f32[30,64,128]{2,1,0:T(8,128)S(1)}, f32[30,64,128]{2,1,0:T(8,128)S(1)}, u32[]{:S(2)}, u32[]{:S(2)}) collective-permute-start(f32[30,64,128]{2,1,0:T(8,128)S(1)} %get-tuple-element.45), channel_id=1, source_target_pairs={{0,4},{1,5},{2,6},{3,7},{4,0},{5,1},{6,2},{7,3},{8,12},{9,13},{10,... | collective-permute-start | bytes 2949128 | tf_op jit(solution)/shard_map/cond/branch_0_fun/ppermute | solution.py:425
  105.1 19.3 %collective-permute-done.14.refs_4_ = f32[30,64,128]{2,1,0:T(8,128)S(1)} collective-permute-done((f32[30,64,128]{2,1,0:T(8,128)S(1)}, f32[30,64,128]{2,1,0:T(8,128)S(1)}, u32[]{:S(2)}, u32[]{:S(2)}) %collective-permute-start.14) | collective-permute-done | bytes 983072 | tf_op jit(solution)/shard_map/cond/branch_0_fun/ppermute | solution.py:425
  124.4 1.7 collective-permute-done.15.refs_5_
  126.1 3.1 step.8
  129.2 9.5 %collective-permute-start.17 = (f32[17,64,128]{2,1,0:T(8,128)}, f32[17,64,128]{2,1,0:T(8,128)}, u32[]{:S(2)}, u32[]{:S(2)}) collective-permute-start(f32[17,64,128]{2,1,0:T(8,128)} %get-tuple-element.52), channel_id=1, source_target_pairs={{0,4},{1,5},{2,6},{3,7},{4,0},{5,1},{6,2},{7,3},{8,12},{9,13},{10,... | collective-permute-start | bytes 1671176 | tf_op jit(solution)/shard_map/cond/branch_0_fun/ppermute | solution.py:425
  138.7 11.8 %multiply.15 = (f32[32,128,128]{2,1,0:T(8,128)S(1)}, f32[32,128,128]{2,1,0:T(8,128)}, s32[1]{0:T(128)}) custom-call(s32[2]{0:T(128)S(1)} %copy-done.6, s32[3,64]{1,0:T(4,128)S(1)} %copy-done.16, s32[22,128]{1,0:T(8,128)S(1)} %copy-done.1, s32[1]{0:T(128)} %get-tuple-element.46.token_ref, f32[8192,1024]{1,0:T(8,128)} %get-tuple-element.25.inverse_ref, ...), custom_call_target="tpu_custom_call" | custom-call | flops 99999997952 | bytes 1 | tf_op jit(solution)/shard_map/cond/branch_0_fun/multiply/pallas_call | solution.py:192
  150.5 11.9 %multiply.16 = (f32[32,128,128]{2,1,0:T(8,128)S(1)}, f32[32,128,128]{2,1,0:T(8,128)}, s32[1]{0:T(128)}) custom-call(s32[2]{0:T(128)S(1)} %copy-done.6, s32[3,64]{1,0:T(4,128)S(1)} %copy-done.16, s32[22,128]{1,0:T(8,128)S(1)} %copy-done.1, s32[1]{0:T(128)} %get-tuple-element.48.token_ref, f32[8192,1024]{1,0:T(8,128)} %get-tuple-element.25.inverse_ref, ...), custom_call_target="tpu_custom_call" | custom-call | flops 99999997952 | bytes 1 | tf_op jit(solution)/shard_map/cond/branch_0_fun/multiply/pallas_call | solution.py:192
  163.1 2.7 step.9
  165.7 11.1 %multiply.17 = (f32[32,128,128]{2,1,0:T(8,128)S(1)}, f32[32,128,128]{2,1,0:T(8,128)S(1)}, s32[1]{0:T(128)}) custom-call(s32[2]{0:T(128)S(1)} %copy-done.6, s32[3,64]{1,0:T(4,128)S(1)} %copy-done.16, s32[22,128]{1,0:T(8,128)S(1)} %copy-done.1, s32[1]{0:T(128)} %get-tuple-element.54.token_ref, f32[8192,1024]{1,0:T(8,128)} %get-tuple-element.25.inverse_ref, ...), custom_call_target="tpu_custom_call" | custom-call | flops 99999997952 | bytes 1 | tf_op jit(solution)/shard_map/cond/branch_0_fun/multiply/pallas_call | solution.py:192
  177.3 2.5 collective-permute-start.23
  181.0 7.2 %merge.5 = (f32[30,64,128]{2,1,0:T(8,128)S(1)}, f32[30,64,128]{2,1,0:T(8,128)S(1)}, f32[30,64,128]{2,1,0:T(8,128)S(1)}, f32[30,64,128]{2,1,0:T(8,128)S(1)}, s32[1]{0:T(128)}) custom-call(s32[22,128]{1,0:T(8,128)S(1)} %copy-done.1, s32[1]{0:T(128)} %get-tuple-element.55.refs_1_, f32[32,128,128]{2,1,0:T(8,128)S(1)} %get-tuple-element.56.refs_2_, ...), custom_call_target="tpu_custom_call" | custom-call | flops 99999997952 | bytes 1 | tf_op jit(solution)/shard_map/cond/branch_0_fun/merge/pallas_call | solution.py:220
  188.3 2.1 collective-permute-start.24
  190.7 11.1 %collective-permute-done.22.refs_6_ = f32[10,64,128]{2,1,0:T(8,128)S(1)} collective-permute-done((f32[10,64,128]{2,1,0:T(8,128)S(1)}, f32[10,64,128]{2,1,0:T(8,128)S(1)}, u32[]{:S(2)}, u32[]{:S(2)}) %collective-permute-start.22) | collective-permute-done | bytes 327712 | tf_op jit(solution)/shard_map/cond/branch_0_fun/ppermute | solution.py:425
  201.8 7.0 %collective-permute-done.23.refs_7_ = f32[10,64,128]{2,1,0:T(8,128)S(1)} collective-permute-done((f32[10,64,128]{2,1,0:T(8,128)S(1)}, f32[10,64,128]{2,1,0:T(8,128)S(1)}, u32[]{:S(2)}, u32[]{:S(2)}) %collective-permute-start.23) | collective-permute-done | bytes 327712 | tf_op jit(solution)/shard_map/cond/branch_0_fun/ppermute | solution.py:425
  208.8 2.2 collect.4
  210.9 1.5 collective-permute-done.24.refs_4_
  212.5 15.4 %collective-permute-done.25.refs_5_ = f32[30,64,128]{2,1,0:T(8,128)S(1)} collective-permute-done((f32[30,64,128]{2,1,0:T(8,128)S(1)}, f32[30,64,128]{2,1,0:T(8,128)S(1)}, u32[]{:S(2)}, u32[]{:S(2)}) %collective-permute-start.25) | collective-permute-done | bytes 983072 | tf_op jit(solution)/shard_map/cond/branch_0_fun/ppermute | solution.py:425
  227.9 2.6 step.10
  231.0 13.0 %collective-permute-done.26.refs_4_ = f32[17,64,128]{2,1,0:T(8,128)S(1)} collective-permute-done((f32[17,64,128]{2,1,0:T(8,128)S(1)}, f32[17,64,128]{2,1,0:T(8,128)S(1)}, u32[]{:S(2)}, u32[]{:S(2)}) %collective-permute-start.26) | collective-permute-done | bytes 557088 | tf_op jit(solution)/shard_map/cond/branch_0_fun/ppermute | solution.py:425
  244.2 2.3 step.11
  247.3 2.1 collective-permute-start.29
  249.4 20.8 %collective-permute-done.28.refs_6_ = f32[10,64,128]{2,1,0:T(8,128)S(1)} collective-permute-done((f32[10,64,128]{2,1,0:T(8,128)S(1)}, f32[10,64,128]{2,1,0:T(8,128)S(1)}, u32[]{:S(2)}, u32[]{:S(2)}) %collective-permute-start.28) | collective-permute-done | bytes 327712 | tf_op jit(solution)/shard_map/cond/branch_0_fun/ppermute | solution.py:425
  270.2 5.9 %collective-permute-done.29.refs_7_ = f32[10,64,128]{2,1,0:T(8,128)S(1)} collective-permute-done((f32[10,64,128]{2,1,0:T(8,128)S(1)}, f32[10,64,128]{2,1,0:T(8,128)S(1)}, u32[]{:S(2)}, u32[]{:S(2)}) %collective-permute-start.29) | collective-permute-done | bytes 327712 | tf_op jit(solution)/shard_map/cond/branch_0_fun/ppermute | solution.py:425
  276.1 2.2 collect.5
  278.4 1.7 collective-permute-done.31.refs_6_
  280.1 4.0 %finish.2 = (f32[512,768]{1,0:T(8,128)}, f32[768,256]{1,0:T(8,128)S(1)}, s32[1]{0:T(128)}) custom-call(s32[2]{0:T(128)S(1)} %copy-done.7, s32[1]{0:T(128)} %get-tuple-element.82.refs_1_, f32[512,768]{1,0:T(8,128)} %get-tuple-element.26.refs_1_.refs_2_, f32[6,128,128]{2,1,0:T(8,128)S(1)} %get-tuple-element.83.refs_3_, ...), custom_call_target="tpu_custom_call" | custom-call | flops 99999997952 | bytes 1 | tf_op jit(solution)/shard_map/cond/branch_0_fun/finish/pallas_call | solution.py:220
  284.3 1.6 collective-permute-done.32
  287.2 2.4 collective-permute-start.34
  289.6 2.1 collective-permute-done.33
  295.6 3.1 collective-permute-start.36
  298.7 3.2 collective-permute-done.38
  301.9 2.5 collective-permute-done.37
  304.5 2.2 collective-permute-start.41
  308.1 2.2 collective-permute-done.41
  310.3 2.0 collective-permute-done.40
  312.7 1.7 collective-permute-done.42
  315.5 2.3 sub.19
  (98 shorter events, 30.0 us)
Async XLA Ops:
  12.0 2.1 collective-permute-start
  12.7 2.1 collective-permute-start.7
  13.4 2.8 collective-permute-start.3
  14.1 3.4 %collective-permute-start.1 = (f32[512,128]{1,0:T(8,128)S(1)}, f32[512,128]{1,0:T(8,128)S(1)}, u32[]{:S(2)}, u32[]{:S(2)}) collective-permute-start(f32[512,128]{1,0:T(8,128)S(1)} %collective-permute-done), channel_id=1, source_target_pairs={{0,0},{1,8},{2,1},{3,9},{4,2},{5,10},{6,3},{7,11},{8,4},{9,12},{10... | collective-permute-start | bytes 786440 | tf_op jit(solution)/shard_map/cond/branch_0_fun/ppermute | solution.py:393
  14.8 23.1 %collective-permute-start.8 = (f32[512,128]{1,0:T(8,128)S(1)}, f32[512,128]{1,0:T(8,128)}, u32[]{:S(2)}, u32[]{:S(2)}) collective-permute-start(f32[512,128]{1,0:T(8,128)S(1)} %collective-permute-done.7), channel_id=1, source_target_pairs={{0,0},{1,8},{2,1},{3,9},{4,2},{5,10},{6,3},{7,11},{8,4},{9,12},{10... | collective-permute-start | bytes 786440 | tf_op jit(solution)/shard_map/cond/branch_0_fun/ppermute | solution.py:393
  16.1 21.9 %collective-permute-start.4 = (f32[512,128]{1,0:T(8,128)S(1)}, f32[512,128]{1,0:T(8,128)}, u32[]{:S(2)}, u32[]{:S(2)}) collective-permute-start(f32[512,128]{1,0:T(8,128)S(1)} %collective-permute-done.3), channel_id=1, source_target_pairs={{0,0},{1,8},{2,1},{3,9},{4,2},{5,10},{6,3},{7,11},{8,4},{9,12},{10... | collective-permute-start | bytes 786440 | tf_op jit(solution)/shard_map/cond/branch_0_fun/ppermute | solution.py:393
  17.5 22.5 %collective-permute-start.2 = (f32[512,128]{1,0:T(8,128)S(1)}, f32[512,128]{1,0:T(8,128)S(1)}, u32[]{:S(2)}, u32[]{:S(2)}) collective-permute-start(f32[512,128]{1,0:T(8,128)S(1)} %collective-permute-done.1.refs_0_), channel_id=1, source_target_pairs={{0,16},{16,0},{1,17},{17,1},{2,18},{18,2},{3,19},{19,3},{4,20},{20... | collective-permute-start | bytes 786440 | tf_op jit(solution)/shard_map/cond/branch_0_fun/ppermute | solution.py:406
  37.9 34.3 %collective-permute-start.9 = (f32[512,128]{1,0:T(8,128)}, f32[512,128]{1,0:T(8,128)}, u32[]{:S(2)}, u32[]{:S(2)}) collective-permute-start(f32[512,128]{1,0:T(8,128)} %collective-permute-done.8.refs_0_), channel_id=1, source_target_pairs={{0,16},{16,0},{1,17},{17,1},{2,18},{18,2},{3,19},{19,3},{4,20},{20... | collective-permute-start | bytes 786440 | tf_op jit(solution)/shard_map/cond/branch_0_fun/ppermute | solution.py:406
  38.0 20.6 %collective-permute-start.5 = (f32[512,128]{1,0:T(8,128)}, f32[512,128]{1,0:T(8,128)}, u32[]{:S(2)}, u32[]{:S(2)}) collective-permute-start(f32[512,128]{1,0:T(8,128)} %collective-permute-done.4.refs_0_), channel_id=1, source_target_pairs={{0,16},{16,0},{1,17},{17,1},{2,18},{18,2},{3,19},{19,3},{4,20},{20... | collective-permute-start | bytes 786440 | tf_op jit(solution)/shard_map/cond/branch_0_fun/ppermute | solution.py:406
  41.4 11.4 %copy-start.13 = (f32[512,768]{1,0:T(8,128)S(1)}, f32[512,768]{1,0:T(8,128)}, u32[]{:S(2)}) copy-start(f32[512,768]{1,0:T(8,128)} %get-tuple-element.26.refs_1_.refs_2_) | copy-start | bytes 4718596 | tf_op jit(solution)/shard_map/cond
  52.7 5.8 %copy-start.1 = (s32[22,128]{1,0:T(8,128)S(1)}, s32[22,128]{1,0:T(8,128)}, u32[]{:S(2)}) copy-start(s32[22,128]{1,0:T(8,128)} %plan.2.table_ref.refs_0_.refs_2_) | copy-start | bytes 33796 | tf_op jit(solution)/shard_map/cond
  54.0 16.9 %collective-permute-start.6 = (f32[512,384]{1,0:T(8,128)S(1)}, f32[512,384]{1,0:T(8,128)S(1)}, u32[]{:S(2)}, u32[]{:S(2)}) collective-permute-start(f32[512,384]{1,0:T(8,128)S(1)} %get-tuple-element.30), channel_id=1, source_target_pairs={{0,0},{1,16},{2,2},{3,18},{4,4},{5,20},{6,6},{7,22},{8,8},{9,24},{... | collective-permute-start | bytes 2359304 | tf_op jit(solution)/shard_map/cond/branch_0_fun/ppermute | solution.py:381
  54.7 30.0 %collective-permute-start.10 = (f32[32,128,128]{2,1,0:T(8,128)}, f32[32,128,128]{2,1,0:T(8,128)}, u32[]{:S(2)}, u32[]{:S(2)}) collective-permute-start(f32[32,128,128]{2,1,0:T(8,128)} %get-tuple-element.36), channel_id=1, source_target_pairs={{0,1},{1,0},{2,3},{3,2},{4,5},{5,4},{6,7},{7,6},{8,9},{9,8},{10,11... | collective-permute-start | bytes 6291464 | tf_op jit(solution)/shard_map/cond/branch_0_fun/ppermute | solution.py:410
  70.8 14.0 %collective-permute-start.11 = (f32[32,128,128]{2,1,0:T(8,128)}, f32[32,128,128]{2,1,0:T(8,128)}, u32[]{:S(2)}, u32[]{:S(2)}) collective-permute-start(f32[32,128,128]{2,1,0:T(8,128)} %get-tuple-element.37), channel_id=1, source_target_pairs={{0,1},{1,0},{2,3},{3,2},{4,5},{5,4},{6,7},{7,6},{8,9},{9,8},{10,11... | collective-permute-start | bytes 6291464 | tf_op jit(solution)/shard_map/cond/branch_0_fun/ppermute | solution.py:410
  83.5 4.3 %collective-permute-start.12 = (f32[32,128,128]{2,1,0:T(8,128)S(1)}, f32[32,128,128]{2,1,0:T(8,128)S(1)}, u32[]{:S(2)}, u32[]{:S(2)}) collective-permute-start(f32[32,128,128]{2,1,0:T(8,128)S(1)} %get-tuple-element.38), channel_id=1, source_target_pairs={{0,1},{1,0},{2,3},{3,2},{4,5},{5,4},{6,7},{7,6},{8,9},{9,8},{10,11... | collective-permute-start | bytes 6291464 | tf_op jit(solution)/shard_map/cond/branch_0_fun/ppermute | solution.py:410
  84.0 19.7 %collective-permute-start.13 = (f32[512,384]{1,0:T(8,128)S(1)}, f32[512,384]{1,0:T(8,128)S(1)}, u32[]{:S(2)}, u32[]{:S(2)}) collective-permute-start(f32[512,384]{1,0:T(8,128)S(1)} %get-tuple-element.40), channel_id=1, source_target_pairs={{0,0},{1,8},{2,1},{3,9},{4,2},{5,10},{6,3},{7,11},{8,4},{9,12},{10... | collective-permute-start | bytes 2359304 | tf_op jit(solution)/shard_map/cond/branch_0_fun/ppermute | solution.py:393
  95.1 29.3 %collective-permute-start.14 = (f32[30,64,128]{2,1,0:T(8,128)S(1)}, f32[30,64,128]{2,1,0:T(8,128)S(1)}, u32[]{:S(2)}, u32[]{:S(2)}) collective-permute-start(f32[30,64,128]{2,1,0:T(8,128)S(1)} %get-tuple-element.44), channel_id=1, source_target_pairs={{0,2},{1,3},{2,0},{3,1},{4,6},{5,7},{6,4},{7,5},{8,10},{9,11},{10,... | collective-permute-start | bytes 2949128 | tf_op jit(solution)/shard_map/cond/branch_0_fun/ppermute | solution.py:425
  97.4 28.7 %collective-permute-start.15 = (f32[30,64,128]{2,1,0:T(8,128)S(1)}, f32[30,64,128]{2,1,0:T(8,128)S(1)}, u32[]{:S(2)}, u32[]{:S(2)}) collective-permute-start(f32[30,64,128]{2,1,0:T(8,128)S(1)} %get-tuple-element.45), channel_id=1, source_target_pairs={{0,4},{1,5},{2,6},{3,7},{4,0},{5,1},{6,2},{7,3},{8,12},{9,13},{10,... | collective-permute-start | bytes 2949128 | tf_op jit(solution)/shard_map/cond/branch_0_fun/ppermute | solution.py:425
  105.0 33.6 %collective-permute-start.16 = (f32[512,384]{1,0:T(8,128)S(1)}, f32[512,384]{1,0:T(8,128)S(1)}, u32[]{:S(2)}, u32[]{:S(2)}) collective-permute-start(f32[512,384]{1,0:T(8,128)S(1)} %get-tuple-element.47.refs_0_), channel_id=1, source_target_pairs={{0,16},{16,0},{1,17},{17,1},{2,18},{18,2},{3,19},{19,3},{4,20},{20... | collective-permute-start | bytes 2359304 | tf_op jit(solution)/shard_map/cond/branch_0_fun/ppermute | solution.py:406
  126.1 12.6 %copy-start.6 = (s32[2]{0:T(128)S(1)}, s32[2]{0:T(128)}, u32[]{:S(2)}) copy-start(s32[2]{0:T(128)} %pad_add_fusion.where_ref.refs_0_) | copy-start | bytes 28 | tf_op jit(solution)/shard_map/cond
  126.1 12.6 %copy-start.16 = (s32[3,64]{1,0:T(4,128)S(1)}, s32[3,64]{1,0:T(4,128)}, u32[]{:S(2)}) copy-start(s32[3,64]{1,0:T(4,128)} %get-tuple-element.24.fill_ref.refs_1_) | copy-start | bytes 2308 | tf_op jit(solution)/shard_map/cond
  129.2 33.9 %collective-permute-start.17 = (f32[17,64,128]{2,1,0:T(8,128)}, f32[17,64,128]{2,1,0:T(8,128)}, u32[]{:S(2)}, u32[]{:S(2)}) collective-permute-start(f32[17,64,128]{2,1,0:T(8,128)} %get-tuple-element.52), channel_id=1, source_target_pairs={{0,4},{1,5},{2,6},{3,7},{4,0},{5,1},{6,2},{7,3},{8,12},{9,13},{10,... | collective-permute-start | bytes 1671176 | tf_op jit(solution)/shard_map/cond/branch_0_fun/ppermute | solution.py:425
  138.6 24.4 %collective-permute-start.18 = (f32[17,64,128]{2,1,0:T(8,128)}, f32[17,64,128]{2,1,0:T(8,128)}, u32[]{:S(2)}, u32[]{:S(2)}) collective-permute-start(f32[17,64,128]{2,1,0:T(8,128)} %get-tuple-element.53), channel_id=1, source_target_pairs={{0,2},{1,3},{2,0},{3,1},{4,6},{5,7},{6,4},{7,5},{8,10},{9,11},{10,... | collective-permute-start | bytes 1671176 | tf_op jit(solution)/shard_map/cond/branch_0_fun/ppermute | solution.py:425
  150.5 29.4 %collective-permute-start.19 = (f32[32,128,128]{2,1,0:T(8,128)}, f32[32,128,128]{2,1,0:T(8,128)}, u32[]{:S(2)}, u32[]{:S(2)}) collective-permute-start(f32[32,128,128]{2,1,0:T(8,128)} %get-tuple-element.59), channel_id=1, source_target_pairs={{0,1},{1,0},{2,3},{3,2},{4,5},{5,4},{6,7},{7,6},{8,9},{9,8},{10,11... | collective-permute-start | bytes 6291464 | tf_op jit(solution)/shard_map/cond/branch_0_fun/ppermute | solution.py:410
  162.5 17.4 %collective-permute-start.20 = (f32[32,128,128]{2,1,0:T(8,128)}, f32[32,128,128]{2,1,0:T(8,128)}, u32[]{:S(2)}, u32[]{:S(2)}) collective-permute-start(f32[32,128,128]{2,1,0:T(8,128)} %get-tuple-element.60), channel_id=1, source_target_pairs={{0,1},{1,0},{2,3},{3,2},{4,5},{5,4},{6,7},{7,6},{8,9},{9,8},{10,11... | collective-permute-start | bytes 6291464 | tf_op jit(solution)/shard_map/cond/branch_0_fun/ppermute | solution.py:410
  176.8 4.2 %collective-permute-start.21 = (f32[32,128,128]{2,1,0:T(8,128)S(1)}, f32[32,128,128]{2,1,0:T(8,128)S(1)}, u32[]{:S(2)}, u32[]{:S(2)}) collective-permute-start(f32[32,128,128]{2,1,0:T(8,128)S(1)} %get-tuple-element.61), channel_id=1, source_target_pairs={{0,1},{1,0},{2,3},{3,2},{4,5},{5,4},{6,7},{7,6},{8,9},{9,8},{10,11... | collective-permute-start | bytes 6291464 | tf_op jit(solution)/shard_map/cond/branch_0_fun/ppermute | solution.py:410
  177.0 24.8 %collective-permute-start.22 = (f32[10,64,128]{2,1,0:T(8,128)S(1)}, f32[10,64,128]{2,1,0:T(8,128)S(1)}, u32[]{:S(2)}, u32[]{:S(2)}) collective-permute-start(f32[10,64,128]{2,1,0:T(8,128)S(1)} %get-tuple-element.65), channel_id=1, source_target_pairs={{0,8},{1,9},{2,10},{3,11},{4,12},{5,13},{6,14},{7,15},{8,0},{9,1},... | collective-permute-start | bytes 983048 | tf_op jit(solution)/shard_map/cond/branch_0_fun/ppermute | solution.py:425
  177.3 31.4 %collective-permute-start.23 = (f32[10,64,128]{2,1,0:T(8,128)S(1)}, f32[10,64,128]{2,1,0:T(8,128)S(1)}, u32[]{:S(2)}, u32[]{:S(2)}) collective-permute-start(f32[10,64,128]{2,1,0:T(8,128)S(1)} %get-tuple-element.66), channel_id=1, source_target_pairs={{0,8},{1,9},{2,10},{3,11},{4,12},{5,13},{6,14},{7,15},{8,0},{9,1},... | collective-permute-start | bytes 983048 | tf_op jit(solution)/shard_map/cond/branch_0_fun/ppermute | solution.py:425
  188.3 24.2 %collective-permute-start.24 = (f32[30,64,128]{2,1,0:T(8,128)S(1)}, f32[30,64,128]{2,1,0:T(8,128)S(1)}, u32[]{:S(2)}, u32[]{:S(2)}) collective-permute-start(f32[30,64,128]{2,1,0:T(8,128)S(1)} %get-tuple-element.70), channel_id=1, source_target_pairs={{0,2},{1,3},{2,0},{3,1},{4,6},{5,7},{6,4},{7,5},{8,10},{9,11},{10,... | collective-permute-start | bytes 2949128 | tf_op jit(solution)/shard_map/cond/branch_0_fun/ppermute | solution.py:425
  190.4 37.5 %collective-permute-start.25 = (f32[30,64,128]{2,1,0:T(8,128)S(1)}, f32[30,64,128]{2,1,0:T(8,128)S(1)}, u32[]{:S(2)}, u32[]{:S(2)}) collective-permute-start(f32[30,64,128]{2,1,0:T(8,128)S(1)} %get-tuple-element.71), channel_id=1, source_target_pairs={{0,4},{1,5},{2,6},{3,7},{4,0},{5,1},{6,2},{7,3},{8,12},{9,13},{10,... | collective-permute-start | bytes 2949128 | tf_op jit(solution)/shard_map/cond/branch_0_fun/ppermute | solution.py:425
  230.5 13.6 %collective-permute-start.26 = (f32[17,64,128]{2,1,0:T(8,128)S(1)}, f32[17,64,128]{2,1,0:T(8,128)S(1)}, u32[]{:S(2)}, u32[]{:S(2)}) collective-permute-start(f32[17,64,128]{2,1,0:T(8,128)S(1)} %get-tuple-element.75), channel_id=1, source_target_pairs={{0,4},{1,5},{2,6},{3,7},{4,0},{5,1},{6,2},{7,3},{8,12},{9,13},{10,... | collective-permute-start | bytes 1671176 | tf_op jit(solution)/shard_map/cond/branch_0_fun/ppermute | solution.py:425
  230.6 13.6 %collective-permute-start.27 = (f32[17,64,128]{2,1,0:T(8,128)S(1)}, f32[17,64,128]{2,1,0:T(8,128)S(1)}, u32[]{:S(2)}, u32[]{:S(2)}) collective-permute-start(f32[17,64,128]{2,1,0:T(8,128)S(1)} %get-tuple-element.76), channel_id=1, source_target_pairs={{0,2},{1,3},{2,0},{3,1},{4,6},{5,7},{6,4},{7,5},{8,10},{9,11},{10,... | collective-permute-start | bytes 1671176 | tf_op jit(solution)/shard_map/cond/branch_0_fun/ppermute | solution.py:425
  244.2 32.0 %copy-start.17 = (s32[3,64]{1,0:T(4,128)S(1)}, s32[3,64]{1,0:T(4,128)}, u32[]{:S(2)}) copy-start(s32[3,64]{1,0:T(4,128)} %get-tuple-element.24.fill_ref.refs_1_) | copy-start | bytes 2308 | tf_op jit(solution)/shard_map/cond
  246.4 23.8 %collective-permute-start.28 = (f32[10,64,128]{2,1,0:T(8,128)S(1)}, f32[10,64,128]{2,1,0:T(8,128)S(1)}, u32[]{:S(2)}, u32[]{:S(2)}) collective-permute-start(f32[10,64,128]{2,1,0:T(8,128)S(1)} %get-tuple-element.80), channel_id=1, source_target_pairs={{0,8},{1,9},{2,10},{3,11},{4,12},{5,13},{6,14},{7,15},{8,0},{9,1},... | collective-permute-start | bytes 983048 | tf_op jit(solution)/shard_map/cond/branch_0_fun/ppermute | solution.py:425
  247.3 28.8 %collective-permute-start.29 = (f32[10,64,128]{2,1,0:T(8,128)S(1)}, f32[10,64,128]{2,1,0:T(8,128)S(1)}, u32[]{:S(2)}, u32[]{:S(2)}) collective-permute-start(f32[10,64,128]{2,1,0:T(8,128)S(1)} %get-tuple-element.81), channel_id=1, source_target_pairs={{0,8},{1,9},{2,10},{3,11},{4,12},{5,13},{6,14},{7,15},{8,0},{9,1},... | collective-permute-start | bytes 983048 | tf_op jit(solution)/shard_map/cond/branch_0_fun/ppermute | solution.py:425
  249.4 29.0 %collective-permute-start.30 = (f32[6,128,128]{2,1,0:T(8,128)S(1)}, f32[6,128,128]{2,1,0:T(8,128)S(1)}, u32[]{:S(2)}, u32[]{:S(2)}) collective-permute-start(f32[6,128,128]{2,1,0:T(8,128)S(1)} %get-tuple-element.84), channel_id=1, source_target_pairs={{0,1},{1,0},{2,3},{3,2},{4,5},{5,4},{6,7},{7,6},{8,9},{9,8},{10,11... | collective-permute-start | bytes 1179656 | tf_op jit(solution)/shard_map/cond/branch_0_fun/ppermute | solution.py:446
  278.3 1.8 collective-permute-start.31
  284.1 1.8 collective-permute-start.32
  286.0 5.7 %collective-permute-start.33 = (f32[96,256]{1,0:T(8,128)S(1)}, f32[96,256]{1,0:T(8,128)S(1)}, u32[]{:S(2)}, u32[]{:S(2)}) collective-permute-start(f32[96,256]{1,0:T(8,128)S(1)} %get-tuple-element.190), channel_id=1, source_target_pairs={{0,2},{1,3},{2,0},{3,1},{4,6},{5,7},{6,4},{7,5},{8,10},{9,11},{10,... | collective-permute-start | bytes 294920 | tf_op jit(solution)/shard_map/cond/branch_0_fun/ppermute | solution.py:332
  287.2 5.6 %collective-permute-start.35 = (f32[96,256]{1,0:T(8,128)S(1)}, f32[96,256]{1,0:T(8,128)S(1)}, u32[]{:S(2)}, u32[]{:S(2)}) collective-permute-start(f32[96,256]{1,0:T(8,128)S(1)} %get-tuple-element.191), channel_id=1, source_target_pairs={{0,18},{1,19},{2,16},{3,17},{4,22},{5,23},{6,20},{7,21},{8,26},{9,... | collective-permute-start | bytes 294920 | tf_op jit(solution)/shard_map/cond/branch_0_fun/ppermute | solution.py:332
  287.2 7.0 %collective-permute-start.34 = (f32[96,256]{1,0:T(8,128)S(1)}, f32[96,256]{1,0:T(8,128)S(1)}, u32[]{:S(2)}, u32[]{:S(2)}) collective-permute-start(f32[96,256]{1,0:T(8,128)S(1)} %get-tuple-element.192), channel_id=1, source_target_pairs={{0,16},{1,17},{2,18},{3,19},{4,20},{5,21},{6,22},{7,23},{8,24},{9,... | collective-permute-start | bytes 294920 | tf_op jit(solution)/shard_map/cond/branch_0_fun/ppermute | solution.py:332
  294.2 7.7 %collective-permute-start.38 = (f32[96,256]{1,0:T(8,128)S(1)}, f32[96,256]{1,0:T(8,128)S(1)}, u32[]{:S(2)}, u32[]{:S(2)}) collective-permute-start(f32[96,256]{1,0:T(8,128)S(1)} %add_add_fusion), channel_id=1, source_target_pairs={{0,12},{1,13},{2,14},{3,15},{4,8},{5,9},{6,10},{7,11},{8,4},{9,5},... | collective-permute-start | bytes 294920 | tf_op jit(solution)/shard_map/cond/branch_0_fun/ppermute | solution.py:332
  295.5 8.9 %collective-permute-start.37 = (f32[96,256]{1,0:T(8,128)S(1)}, f32[96,256]{1,0:T(8,128)S(1)}, u32[]{:S(2)}, u32[]{:S(2)}) collective-permute-start(f32[96,256]{1,0:T(8,128)S(1)} %add_add_fusion), channel_id=1, source_target_pairs={{0,8},{1,9},{2,10},{3,11},{4,12},{5,13},{6,14},{7,15},{8,0},{9,1},... | collective-permute-start | bytes 294920 | tf_op jit(solution)/shard_map/cond/branch_0_fun/ppermute | solution.py:332
  295.6 8.9 %collective-permute-start.36 = (f32[96,256]{1,0:T(8,128)S(1)}, f32[96,256]{1,0:T(8,128)S(1)}, u32[]{:S(2)}, u32[]{:S(2)}) collective-permute-start(f32[96,256]{1,0:T(8,128)S(1)} %add_add_fusion), channel_id=1, source_target_pairs={{0,4},{1,5},{2,6},{3,7},{4,0},{5,1},{6,2},{7,3},{8,12},{9,13},{10,... | collective-permute-start | bytes 294920 | tf_op jit(solution)/shard_map/cond/branch_0_fun/ppermute | solution.py:332
  304.5 5.8 %collective-permute-start.41 = (f32[96,256]{1,0:T(8,128)S(1)}, f32[96,256]{1,0:T(8,128)S(1)}, u32[]{:S(2)}, u32[]{:S(2)}) collective-permute-start(f32[96,256]{1,0:T(8,128)S(1)} %fusion.23), channel_id=1, source_target_pairs={{0,18},{1,19},{2,16},{3,17},{4,22},{5,23},{6,20},{7,21},{8,26},{9,... | collective-permute-start | bytes 294920 | tf_op jit(solution)/shard_map/cond/branch_0_fun/ppermute | solution.py:332
  306.8 5.6 %collective-permute-start.40 = (f32[96,256]{1,0:T(8,128)S(1)}, f32[96,256]{1,0:T(8,128)S(1)}, u32[]{:S(2)}, u32[]{:S(2)}) collective-permute-start(f32[96,256]{1,0:T(8,128)S(1)} %fusion.23), channel_id=1, source_target_pairs={{0,16},{1,17},{2,18},{3,19},{4,20},{5,21},{6,22},{7,23},{8,24},{9,... | collective-permute-start | bytes 294920 | tf_op jit(solution)/shard_map/cond/branch_0_fun/ppermute | solution.py:332
  307.3 5.2 %collective-permute-start.39 = (f32[96,256]{1,0:T(8,128)S(1)}, f32[96,256]{1,0:T(8,128)S(1)}, u32[]{:S(2)}, u32[]{:S(2)}) collective-permute-start(f32[96,256]{1,0:T(8,128)S(1)} %fusion.23), channel_id=1, source_target_pairs={{0,2},{1,3},{2,0},{3,1},{4,6},{5,7},{6,4},{7,5},{8,10},{9,11},{10,... | collective-permute-start | bytes 294920 | tf_op jit(solution)/shard_map/cond/branch_0_fun/ppermute | solution.py:332
  312.7 1.8 collective-permute-start.42
  (5 other events, 17.0 us)

commit v2 on v1

v2 whole, which is shorter than its diff:
```python
import functools

import jax
import jax.numpy as jnp
import numpy as np
from jax import lax
from jax.experimental import pallas as pl
from jax.experimental.pallas import tpu as pltpu
from jax.sharding import PartitionSpec as P

W = 256
SIBS = 3
TILE = 256
VMEM_LIMIT = 32 * 1024 * 1024
MULTIPLY_VMEM = 32 * 1024 * 1024
STRIPS = (((0, 2, 0), (2, 4, 1)), ((0, 2, 0), (2, 4, 1)), ((0, 2, 0), (2, 4, 1)))
SLOTS = 6
TOKEN = jax.ShapeDtypeStruct((1,), jnp.int32)
LONG = pl.CostEstimate(flops=10**11, bytes_accessed=1, transcendentals=0)
SMEM = pltpu.SMEM
VMEM = pltpu.VMEM


class Plan:
    def __init__(self, row_devices, col_devices, own_rows, band_rows, block_rows):
        self.row_devices, self.col_devices = row_devices, col_devices
        self.own_rows, self.band_rows, self.block_rows = own_rows, band_rows, block_rows
        self.bits = col_devices.bit_length() - 1
        self.high = min(TILE, own_rows)
        self.half = self.high // 2
        self.sub = TILE // self.high
        self.per = own_rows // self.high
        self.tile_rows = band_rows // self.high
        self.blocks = band_rows // TILE
        first = list(range(1, self.bits))
        second = [2, 1] + first[2:] if self.bits > 2 else first
        self.steps = len(first)
        self.orders = (first, second)
        unit = self.half // 4
        self.strips = [[(a * unit, b * unit, order) for a, b, order in sibling] for sibling in STRIPS]
        every = [(order, step) for order in range(2) for step in range(self.steps)]
        self.sequences = list({self.sequence(*each): each for each in every}.values())

    @property
    def table_rows(self):
        return 3 + 6 * self.steps

    def block_row(self, k):
        return k * self.table_rows

    def rank_row(self, k):
        return k * self.table_rows + 1

    def count_row(self, k):
        return k * self.table_rows + 2

    def sequence(self, order, step):
        same = self.orders[0] == self.orders[1] or step > 1
        return (0 if same else order) * self.steps + step

    def pos_row(self, k, order, step):
        return k * self.table_rows + 3 + 3 * self.sequence(order, step)

    def give_row(self, k, order, step):
        return 1 + self.pos_row(k, order, step)

    def hold_row(self, k, order, step):
        return 2 + self.pos_row(k, order, step)

    def give_count(self, order, step):
        return 1 + 2 * self.sequence(order, step)

    def hold_count(self, order, step):
        return 1 + self.give_count(order, step)


def plan_kernel(plan, where_ref, fill_ref, table_ref):
    row_index, col_index = where_ref[0], where_ref[1]
    sequences = plan.sequences
    zero = jnp.int32(0)

    def one_sibling(k, carry):
        def one_block(block, count):
            table_ref[plan.block_row(k), count] = block
            table_ref[plan.rank_row(k), block] = count
            return count + fill_ref[k, row_index * plan.blocks + block]

        table_ref[plan.count_row(k), 0] = lax.fori_loop(0, plan.blocks, one_block, zero)

        def one_tile(tile, counts):
            apart = (tile // plan.per) ^ col_index

            def place(counts):
                result = []
                for number, (order, step) in enumerate(sequences):
                    held, sent = counts[2 * number], counts[2 * number + 1]
                    bits = plan.orders[order]
                    earlier = sum(1 << bit for bit in bits[:step])
                    here = 1 << bits[step]
                    table_ref[plan.pos_row(k, order, step), tile] = held
                    table_ref[plan.hold_row(k, order, step), held] = tile
                    table_ref[plan.give_row(k, order, step), sent] = tile
                    keeps = (apart & (earlier | here)) == 0
                    gives = (apart & (earlier | here)) == here
                    result += [held + keeps.astype(jnp.int32), sent + gives.astype(jnp.int32)]
                return tuple(result)

            active = fill_ref[k, (row_index * plan.tile_rows + tile) // plan.sub] != 0
            return lax.cond(active, place, lambda counts: counts, counts)

        counts = lax.fori_loop(0, plan.tile_rows, one_tile, (zero,) * (2 * len(sequences)))
        for number, (order, step) in enumerate(sequences):
            table_ref[plan.count_row(k), plan.hold_count(order, step)] = counts[2 * number]
            table_ref[plan.count_row(k), plan.give_count(order, step)] = counts[2 * number + 1]
        return carry

    lax.fori_loop(0, SIBS, one_sibling, zero)


def make_plan(plan, where, fill_list):
    width = -(-max(plan.tile_rows + 1, 3 + 4 * plan.steps) // 128) * 128
    return pl.pallas_call(
        functools.partial(plan_kernel, plan),
        out_shape=jax.ShapeDtypeStruct((SIBS * plan.table_rows, width), jnp.int32),
        in_specs=[pl.BlockSpec(memory_space=SMEM)] * 2,
        out_specs=pl.BlockSpec(memory_space=SMEM),
        name="plan",
    )(where, fill_list)


def split_high_low(values):
    high = values.astype(jnp.bfloat16)
    return high, (values - high.astype(jnp.float32)).astype(jnp.bfloat16)


def multiply_kernel(plan, k, ahead, where_ref, fill_ref, table_ref, token_ref, inverse_ref, *refs):
    pieces, refs = refs[: plan.row_devices], refs[plan.row_devices + ahead :]
    keep_ref, send_ref, done_ref, upper_ref, lower_ref, rows_ref, both_ref, total_ref, sems = refs
    done_ref[0] = token_ref[0]
    row_index, col_index = where_ref[0], where_ref[1]
    core = col_index % 2
    count = table_ref[plan.count_row(k), 0]

    def fetch(number, slot):
        start = pl.multiple_of(table_ref[plan.block_row(k), number] * TILE, TILE)
        return pltpu.make_async_copy(inverse_ref.at[pl.ds(start, TILE), :], rows_ref.at[slot], sems.at[slot])

    for number in range(SLOTS - 1):

        @pl.when(number < count)
        def _(number=number):
            fetch(number, number).start()

    for shift in range(plan.row_devices):
        source = lax.rem(row_index - shift + plan.row_devices, plan.row_devices)
        for part in range(plan.per):
            start = pl.multiple_of(source * plan.own_rows + part * plan.high, plan.high)
            filled = fill_ref[k, (col_index * plan.block_rows + start) // TILE].astype(jnp.float32)
            high, low = split_high_low(pieces[shift][part * plan.high : (part + 1) * plan.high, :] * filled)
            upper_ref[pl.ds(start, plan.high), :] = high
            lower_ref[pl.ds(start, plan.high), :] = low

    def one(number, carry):
        slot = lax.rem(number, SLOTS)
        fetch(number, slot).wait()

        @pl.when(number + SLOTS - 1 < count)
        def _():
            fetch(number + SLOTS - 1, lax.rem(number + SLOTS - 1, SLOTS)).start()

        high, low = split_high_low(rows_ref[slot])
        both_ref[:TILE] = high
        both_ref[TILE:] = low
        first = jnp.dot(both_ref[...], upper_ref[...], preferred_element_type=jnp.float32)
        second = jnp.dot(both_ref[:TILE], lower_ref[...], preferred_element_type=jnp.float32)
        total_ref[...] = first[:TILE] + (first[TILE:] + second)
        for part in range(plan.sub):
            near = pl.multiple_of(part * plan.high + core * plan.half, plan.half)
            far = pl.multiple_of(part * plan.high + (1 - core) * plan.half, plan.half)
            keep_ref[number * plan.sub + part] = total_ref[pl.ds(near, plan.half), :]
            send_ref[number * plan.sub + part] = total_ref[pl.ds(far, plan.half), :]
        return carry

    lax.fori_loop(0, count, one, 0)


def multiply(plan, cap, k, where, fill_list, table, token, inverse, pieces, ahead):
    shape = jax.ShapeDtypeStruct((cap, plan.half, W), jnp.float32)
    smem, vmem, anywhere = (pl.BlockSpec(memory_space=space) for space in (SMEM, VMEM, pl.ANY))
    return pl.pallas_call(
        functools.partial(multiply_kernel, plan, k, len(ahead)),
        out_shape=(shape, shape, TOKEN),
        in_specs=[smem] * 4 + [anywhere] + [vmem] * len(pieces) + [anywhere] * len(ahead),
        out_specs=(vmem, vmem, smem),
        scratch_shapes=[
            VMEM((plan.block_rows, W), jnp.bfloat16),
            VMEM((plan.block_rows, W), jnp.bfloat16),
            VMEM((SLOTS, TILE, plan.block_rows), jnp.float32),
            VMEM((2 * TILE, plan.block_rows), jnp.bfloat16),
            VMEM((TILE, W), jnp.float32),
            pltpu.SemaphoreType.DMA((SLOTS,)),
        ],
        compiler_params=pltpu.CompilerParams(vmem_limit_bytes=MULTIPLY_VMEM),
        cost_estimate=LONG,
        name="multiply",
    )(where, fill_list, table, token, inverse, *pieces, *ahead)


def call_local(kernel, out_shape, tables, token, operands, name, scratch=(), ahead=()):
    vmem, smem = pl.BlockSpec(memory_space=VMEM), pl.BlockSpec(memory_space=SMEM)

    def body(*refs):
        tables_in, token_ref, rest = refs[: len(tables)], refs[len(tables)], refs[len(tables) + len(ahead) + 1 :]
        last = len(operands) + len(out_shape)
        rest[last][0] = token_ref[0]
        kernel(*tables_in, *rest[:last], *rest[last + 1 :])

    return pl.pallas_call(
        body,
        out_shape=tuple(jax.ShapeDtypeStruct(x.shape, x.dtype) for x in out_shape) + (TOKEN,),
        in_specs=[smem] * (len(tables) + 1) + [pl.BlockSpec(memory_space=pl.ANY)] * len(ahead) + [vmem] * len(operands),
        out_specs=(vmem,) * len(out_shape) + (smem,),
        scratch_shapes=scratch,
        compiler_params=pltpu.CompilerParams(vmem_limit_bytes=VMEM_LIMIT),
        cost_estimate=LONG,
        name=name,
    )(*tables, token, *ahead, *operands)


def tile_lists(plan, table_ref, k, step, order, outs):
    counts = plan.count_row(k)
    yield outs[0], plan.give_row(k, order, step), table_ref[counts, plan.give_count(order, step)]
    yield outs[1], plan.hold_row(k, order, step), table_ref[counts, plan.hold_count(order, step)]


def relay_kernel(in_ref, out_ref):
    out_ref[...] = in_ref[...]


def merge_kernel(plan, k, table_ref, keep_ref, core_ref, *outs):
    for number, (first, last, order) in enumerate(plan.strips[k]):
        for out_ref, row, count in tile_lists(plan, table_ref, k, 0, order, outs[2 * number : 2 * number + 2]):

            def one(slot, carry, out_ref=out_ref, row=row, first=first, last=last):
                tile = table_ref[row, slot]
                place = table_ref[plan.rank_row(k), tile // plan.sub] * plan.sub + tile % plan.sub
                out_ref[slot] = keep_ref[place, first:last, :] + core_ref[place, first:last, :]
                return carry

            lax.fori_loop(0, count, one, 0)


def step_kernel(plan, k, step, table_ref, *refs):
    strips = plan.strips[k]
    size = len(strips)
    for number, (_, _, order) in enumerate(strips):
        held_ref, came_ref = refs[number], refs[size + number]
        outs = refs[2 * size + 2 * number : 2 * size + 2 * number + 2]
        for out_ref, row, count in tile_lists(plan, table_ref, k, step, order, outs):

            def one(slot, carry, out_ref=out_ref, row=row, order=order, held_ref=held_ref, came_ref=came_ref):
                place = table_ref[plan.pos_row(k, order, step - 1), table_ref[row, slot]]
                out_ref[slot] = held_ref[place] + came_ref[place]
                return carry

            lax.fori_loop(0, count, one, 0)


def strip_shapes(cap, strip):
    return (jax.ShapeDtypeStruct((cap, strip[1] - strip[0], W), jnp.float32),) * 2


def collect_kernel(plan, k, where_ref, fill_ref, table_ref, *refs):
    strips = plan.strips[k]
    size = len(strips)
    held, came, (near_ref, far_ref) = refs[:size], refs[size : 2 * size], refs[2 * size :]
    row_index, col_index = where_ref[0], where_ref[1]
    for out_ref, owner in ((near_ref, col_index), (far_ref, col_index ^ 1)):
        for part in range(plan.per):
            tile = owner * plan.per + part
            active = fill_ref[k, (row_index * plan.tile_rows + tile) // plan.sub] != 0

            @pl.when(active)
            def _(out_ref=out_ref, tile=tile, part=part):
                for number, (first, last, order) in enumerate(strips):
                    source = table_ref[plan.pos_row(k, order, plan.steps - 1), tile]
                    out_ref[part, first:last, :] = -(held[number][source] + came[number][source])

            @pl.when(jnp.logical_not(active))
            def _(out_ref=out_ref, part=part):
                out_ref[part] = jnp.zeros(out_ref.shape[1:], jnp.float32)


def finish_kernel(plan, where_ref, factor_ref, *refs):
    parts, (block_ref, term_ref) = refs[: 2 * SIBS], refs[2 * SIBS :]
    core = where_ref[1] % 2
    for k in range(SIBS):
        near_ref, far_ref = parts[2 * k], parts[2 * k + 1]
        columns = slice(k * W, (k + 1) * W)
        for part in range(plan.per):
            near = pl.multiple_of(part * plan.high + core * plan.half, plan.half)
            far = pl.multiple_of(part * plan.high + (1 - core) * plan.half, plan.half)
            block_ref[pl.ds(near, plan.half), columns] = near_ref[part]
            block_ref[pl.ds(far, plan.half), columns] = far_ref[part]
        term_ref[columns, :] = lax.dot_general(
            factor_ref[:, columns],
            block_ref[:, columns],
            (((0,), (0,)), ((), ())),
            precision=lax.Precision.HIGHEST,
            preferred_element_type=jnp.float32,
        )


def toggled(value, mask, devices):
    return lax.ppermute(value, ("row", "col"), [(i, i ^ mask) for i in range(devices)])


def minus_sum_everywhere(plan, base, value):
    cols, devices = plan.col_devices, plan.row_devices * plan.col_devices
    me = lax.axis_index("row") * cols + lax.axis_index("col")
    masks = [1 << bit for bit in range(devices.bit_length() - 1)]
    row_masks = [m for m in masks if m >= cols]
    col_masks = [m for m in masks if m < cols]
    rest = col_masks[2:] + row_masks[1:]
    groups = [col_masks[:1], col_masks[1:2] + row_masks[:1]]
    groups += [rest[i : i + 2] for i in range(0, len(rest), 2)]

    def member(group):
        return sum(((me & mask) != 0).astype(jnp.int32) << n for n, mask in enumerate(group))

    def spread(group, number):
        return sum(mask for n, mask in enumerate(group) if number >> n & 1)

    for group in groups[:-1]:
        size = 1 << len(group)
        rows = value.shape[0] // size
        mine = member(group)
        sent = [
            toggled(lax.dynamic_slice_in_dim(value, (mine ^ d) * rows, rows, 0), spread(group, d), devices)
            for d in range(1, size)
        ]
        own = lax.dynamic_slice_in_dim(value, mine * rows, rows, 0)
        value = functools.reduce(jnp.add, sent, own)
        base = lax.dynamic_slice_in_dim(base, mine * rows, rows, 0)
    group = groups[-1]
    arrived = [toggled(value, spread(group, d), devices) for d in range(1, 1 << len(group))]
    mine = member(group)
    whole = jnp.stack([value] + arrived)
    ordered = [lax.dynamic_index_in_dim(whole, mine ^ n, 0, False) for n in range(1 << len(group))]
    value = base - functools.reduce(jnp.add, ordered)
    for group in reversed(groups[:-1]):
        size = 1 << len(group)
        mine = member(group)
        parts = [value] + [toggled(value, spread(group, d), devices) for d in range(1, size)]
        whole = jnp.stack(parts)
        value = jnp.concatenate([lax.dynamic_index_in_dim(whole, mine ^ n, 0, False) for n in range(size)])
    return value


def cross(plan, value):
    rows, cols = plan.row_devices, plan.col_devices
    if rows != 2:
        return value
    pairs = [(r * cols + c, (c & 1) * cols + (c & ~1 | r)) for r in range(rows) for c in range(cols)]
    return lax.ppermute(value, ("row", "col"), pairs)


def home(plan, value):
    rows, cols = plan.row_devices, plan.col_devices
    if rows != 2:
        pairs = [(rows * j + h, h * cols + j) for j in range(cols) for h in range(rows)]
    else:
        pairs = []
        for y in range(rows):
            for c in range(cols):
                pairs.append((y * cols + c, y * cols + ((c & 1) * cols + (c & ~1 | y)) // 2))
    return lax.ppermute(value, ("row", "col"), pairs)


def sparse(plan, caps, ancestor_inv, factor_rows, diagonal_inv, fill_list):
    rows, cols = plan.row_devices, plan.col_devices
    where = jnp.stack([lax.axis_index("row"), lax.axis_index("col")]).astype(jnp.int32)
    table = make_plan(plan, where, fill_list)
    pair = [(i, i ^ 1) for i in range(cols)]
    turns = [[(i, (i + shift) % rows) for i in range(rows)] for shift in range(1, rows)]
    tile_set = jax.ShapeDtypeStruct((plan.per, plan.half, W), jnp.float32)
    crossed = [cross(plan, factor_rows[:, k * W : (k + 1) * W]) for k in range(SIBS)]
    homes = [home(plan, value) for value in crossed]
    state = [None] * SIBS

    def exchange(k, number, made):
        held, came = [], []
        for n, strip in enumerate(plan.strips[k]):
            bit = 1 << plan.orders[strip[2]][number]
            came.append(lax.ppermute(made[2 * n], "col", [(i, i ^ bit) for i in range(cols)]))
            held.append(made[2 * n + 1])
        state[k] = held + came

    def product(k, token):
        pieces = [homes[k]] + [lax.ppermute(homes[k], "row", turn) for turn in turns]
        ahead = homes[1:2] + crossed[2:3] if k == 0 else []
        near, far, token = multiply(
            plan, caps[0], k, where, fill_list, table, token, ancestor_inv, pieces, ahead
        )
        state[k] = [near, lax.ppermute(far, "col", pair)]
        return token

    def merge(k, token):
        shapes = sum((strip_shapes(caps[1], strip) for strip in plan.strips[k]), ())
        *made, token = call_local(functools.partial(merge_kernel, plan, k), shapes, [table], token, state[k], "merge")
        exchange(k, 0, made)
        return token

    def step(k, number, token):
        shapes = sum((strip_shapes(caps[number + 1], strip) for strip in plan.strips[k]), ())
        kernel = functools.partial(step_kernel, plan, k, number)
        *made, token = call_local(kernel, shapes, [table], token, state[k], "step")
        exchange(k, number, made)
        return token

    def collect(k, token):
        kernel = functools.partial(collect_kernel, plan, k)
        tables = [where, fill_list, table]
        near, far, token = call_local(kernel, (tile_set, tile_set), tables, token, state[k], "collect")
        state[k] = [near, lax.ppermute(far, "col", pair)]
        return token

    token = jnp.zeros(TOKEN.shape, TOKEN.dtype)
    last = plan.steps - 1
    token = product(0, token)
    token = merge(0, token)
    homes[2], token = call_local(relay_kernel, (homes[2],), [], token, [homes[2]], "relay")
    token = product(1, token)
    token = step(0, 1, token)
    token = merge(1, token)
    token = product(2, token)
    token = step(0, 2, token)
    token = step(1, 1, token)
    token = merge(2, token)
    for number in range(3, plan.steps):
        token = step(0, number, token)
        token = step(1, number - 1, token)
        token = step(2, number - 2, token)
    token = collect(0, token)
    token = step(1, last, token)
    token = step(2, last - 1, token)
    token = collect(1, token)
    token = step(2, last, token)
    token = collect(2, token)
    shapes = (
        jax.ShapeDtypeStruct(factor_rows.shape, jnp.float32),
        jax.ShapeDtypeStruct((SIBS * W, W), jnp.float32),
    )
    kernel = functools.partial(finish_kernel, plan)
    column_block, term, _ = call_local(kernel, shapes, [where], token, [factor_rows] + sum(state, []), "finish")
    diagonal_block = minus_sum_everywhere(plan, diagonal_inv.reshape(term.shape), term)
    return column_block, diagonal_block.reshape(diagonal_inv.shape)


def row_masks(fill_list, first_row, row_count):
    positions = first_row + jnp.arange(row_count, dtype=jnp.int32)
    tile_index = positions // TILE
    one_hot = (
        tile_index[:, None] == jnp.arange(fill_list.shape[1], dtype=jnp.int32)[None, :]
    ).astype(jnp.float32)
    return jnp.dot(one_hot, fill_list.T.astype(jnp.float32), precision=lax.Precision.HIGHEST)


def dense(ancestor_inv, factor_rows, diagonal_inv, fill_list):
    row_devices, col_devices = lax.axis_size("row"), lax.axis_size("col")
    group_span = col_devices // row_devices
    own_rows = factor_rows.shape[0]
    band_rows, block_rows = ancestor_inv.shape
    row_index, col_index = lax.axis_index("row"), lax.axis_index("col")
    first_row = row_index * band_rows + col_index * own_rows
    wide_mask = jnp.repeat(row_masks(fill_list, first_row, own_rows), W, axis=1)
    masked = factor_rows * wide_mask
    band = lax.all_gather(masked, "col", axis=0, tiled=True)
    section = lax.dynamic_slice_in_dim(band, col_index % group_span * block_rows, block_rows, 0)
    section = jnp.where(row_index == col_index // group_span, section, jnp.zeros_like(section))
    product = jnp.dot(ancestor_inv, lax.psum(section, "row"), precision=lax.Precision.HIGHEST)
    summed = lax.psum_scatter(product, "col", scatter_dimension=0, tiled=True)
    column_block = -summed * wide_mask
    left_side = masked.reshape(own_rows, SIBS, W)
    right_side = column_block.reshape(own_rows, SIBS, W)
    local_term = jnp.einsum("rkw,rkv->kwv", left_side, right_side, precision=lax.Precision.HIGHEST)
    update = lax.psum(local_term, ("row", "col"))
    return column_block, diagonal_inv - update


def fill_groups(plan):
    devices = np.arange(plan.row_devices * plan.col_devices)
    found = {}
    for order in plan.orders:
        for step in range(plan.steps + 1):
            mask = sum(1 << bit for bit in order[:step])
            key = (devices // plan.col_devices) * plan.col_devices + (devices % plan.col_devices & mask)
            for value in np.unique(key):
                found[(key == value).tobytes()] = (key == value, step)
    member = np.stack([group for group, _ in found.values()], axis=1).astype(np.float32)
    return np.repeat(member, plan.per, axis=0), np.array([step for _, step in found.values()])


SHARES = (((22, 32), (12, 16), (7, 8), (4, 4), (2, 2)), ((26, 32), (14, 16), (8, 8), (4, 4), (2, 2)))


def local(ancestor_inv, factor_rows, diagonal_inv, fill_list):
    plan = Plan(
        lax.axis_size("row"), lax.axis_size("col"), factor_rows.shape[0], ancestor_inv.shape[0], ancestor_inv.shape[1]
    )
    member, levels = fill_groups(plan)
    block_of = np.arange(member.shape[0]) // plan.sub
    spread = np.zeros((fill_list.shape[1], member.shape[1]), np.float32)
    np.add.at(spread, block_of, member)
    found = jnp.dot(fill_list.astype(jnp.float32), spread, precision=lax.Precision.HIGHEST)
    limits, branches = [], []
    for shares in SHARES:
        caps = []
        for level in range(plan.steps + 1):
            size = plan.tile_rows >> level
            part, full = shares[min(level, len(shares) - 1)]
            caps.append(min(size, -(-size * part // full)))
        limits.append([caps[level] for level in levels])
        branches.append(functools.partial(sparse, plan, caps))
    branches.append(dense)
    over = jnp.any(found[None] > np.array(limits, np.float32)[:, None], axis=(1, 2))
    index = jnp.sum(over.astype(jnp.int32))
    return lax.switch(index, branches, ancestor_inv, factor_rows, diagonal_inv, fill_list)


def solution(mesh):
    placed = (P("row", "col"), P(("row", "col"), None), P(), P())
    return jax.shard_map(
        local, mesh=mesh, in_specs=placed, out_specs=(P(("row", "col"), None), P()), check_vma=False
    )
```

time: 324 us -> 279 us (0.86)
  Pallas kernels: 114 us -> 85.9 us
  waiting for transfers between devices: 120 us -> 96.7 us
  starting transfers between devices: 65.4 us -> 72.9 us
    pallas_call x18 -> x17, Pallas kernels: 107 us -> 78.9 us  [the longest x3 39.8 us: multiply(): pl.pallas_call(functools.partial(multiply_kernel, plan, k, len(ahead)), o...]
    ppermute x24 -> x27, waiting for transfers between devices: 102 us -> 77.7 us  [the longest x18 66.1 us: exchange(): lax.ppermute(made[2 * n], 'col', [(i, i ^ bit) for i in range(cols)])]
    ppermute x24 -> x27, starting transfers between devices: 46.7 us -> 56.1 us  [the longest x18 36.4 us: exchange(): lax.ppermute(made[2 * n], 'col', [(i, i ^ bit) for i in range(cols)])]
  transfers between devices with their start and end apart: 43 -> 44, of which waited for: 23 -> 25; matrix products, arithmetic and copies ran while one was open for 0% -> 0% of each run, Pallas kernels for 32% -> 24%
where the time goes in v2:
time: 279 us
  waiting for transfers between devices  96.7 us (35%)
  Pallas kernels  85.9 us (31%)
  starting transfers between devices  72.9 us (26%)
  between operations  14.7 us (5%)
  other arithmetic  4.25 us (2%)
  local copies, waits for them, and re-layouts  2.97 us (1%)
    ppermute x18, waiting for transfers between devices, exchange(): lax.ppermute(made[2 * n], 'col', [(i, i ^ bit) for i in range(cols)])  66.1 us
    pallas_call x3, Pallas kernels, multiply(): pl.pallas_call(functools.partial(multiply_kernel, plan, k, len(ahead)), o...  39.8 us
    pallas_call x14, Pallas kernels, call_local(): pl.pallas_call(body, out_shape=tuple((jax.ShapeDtypeStruct(x.shape, x.dty...  39 us
    ppermute x18, starting transfers between devices, exchange(): lax.ppermute(made[2 * n], 'col', [(i, i ^ bit) for i in range(cols)])  36.4 us
    ppermute x11, waiting for transfers between devices, toggled(): lax.ppermute(value, ('row', 'col'), [(i, i ^ mask) for i in range(devices)])  19 us
    ppermute x3, starting transfers between devices, product(): lax.ppermute(homes[k], 'row', turn)  18.2 us
    ppermute x11, starting transfers between devices, toggled(): lax.ppermute(value, ('row', 'col'), [(i, i ^ mask) for i in range(devices)])  11.8 us
    pallas_call x1, Pallas kernels, make_plan(): pl.pallas_call(functools.partial(plan_kernel, plan), out_shape=jax.ShapeD...  7.01 us
  transfers between devices with their start and end apart: 44, of which 25 were waited for; matrix products, arithmetic and copies ran while one was open for 0% of the time, Pallas kernels for 24%

profile of v2, /device:TPU:0, one launch (start us, length us, event | category | flops | bytes accessed | tf_op | source)
XLA Modules:
  0.0 278.7 jit_solution(3681014341917756678)
XLA Ops:
  10.2 261.7 %conditional.1 = (f32[512,768]{1,0:T(8,128)}, f32[3,256,256]{2,1,0:T(8,128)}) conditional(s32[]{:T(128)} %clamp.11, (s32[3,64]{1,0:T(4,128)}, f32[512,768]{1,0:T(8,128)}, f32[8192,1024]{1,0:T(8,128)}, f32[3,256,256]{2,1,0:T(8,128)}) %tuple.19, (s32[3,64]{1,0:T(4,128)}, f32[512,768]{1,0:T(8,128)}, f32[8192,1024]{1,0:T(8,128)}, ...), branch_computations={%region_2.3_spmd, %region_3.4_spmd, %region_4.8_spmd} | conditional | flops 1700001218560 | bytes 280521024 | solution.py:528
  16.0 16.2 %collective-permute-start.2 = (f32[512,256]{1,0:T(8,128)S(1)}, f32[512,256]{1,0:T(8,128)S(1)}, u32[]{:S(2)}, u32[]{:S(2)}) collective-permute-start(f32[512,256]{1,0:T(8,128)S(1)} %collective-permute-done.1.refs_0_), channel_id=1, source_target_pairs={{0,16},{16,0},{1,17},{17,1},{2,18},{18,2},{3,19},{19,3},{4,20},{20... | collective-permute-start | bytes 1572872 | tf_op jit(solution)/shard_map/cond/branch_0_fun/ppermute | solution.py:400
  32.8 7.0 %plan.2.table_ref.refs_0_.refs_2_ = s32[63,128]{1,0:T(8,128)} custom-call(s32[2]{0:T(128)} %pad_add_fusion.where_ref.refs_0_, s32[3,64]{1,0:T(4,128)S(1)} %copy-done.14), custom_call_target="tpu_custom_call" | custom-call | tf_op jit(solution)/shard_map/cond/branch_0_fun/plan/pallas_call | solution.py:122
  39.8 6.8 %collective-permute-done.2.refs_1_ = f32[512,256]{1,0:T(8,128)S(1)} collective-permute-done((f32[512,256]{1,0:T(8,128)S(1)}, f32[512,256]{1,0:T(8,128)S(1)}, u32[]{:S(2)}, u32[]{:S(2)}) %collective-permute-start.2) | collective-permute-done | bytes 524320 | tf_op jit(solution)/shard_map/cond/branch_0_fun/ppermute | solution.py:400
  48.0 12.8 %multiply.6 = (f32[22,128,256]{2,1,0:T(8,128)S(1)}, f32[22,128,256]{2,1,0:T(8,128)S(1)}, s32[1]{0:T(128)}) custom-call(s32[2]{0:T(128)S(1)} %copy-done.4, s32[3,64]{1,0:T(4,128)S(1)} %copy-done.14, s32[63,128]{1,0:T(8,128)S(1)} %copy-done, s32[1]{0:T(128)} %constant.148.clone.token_ref, f32[8192,1024]{1,0:T(8,128)} %get-tuple-element.185.inverse_ref, ...), custom_call_target="tpu_custom_call" | custom-call | flops 99999997952 | bytes 1 | tf_op jit(solution)/shard_map/cond/branch_0_fun/multiply/pallas_call | solution.py:190
  63.0 3.3 %collective-permute-done.6.refs_3_ = f32[22,128,256]{2,1,0:T(8,128)S(1)} collective-permute-done((f32[22,128,256]{2,1,0:T(8,128)S(1)}, f32[22,128,256]{2,1,0:T(8,128)S(1)}, u32[]{:S(2)}, u32[]{:S(2)}) %collective-permute-start.6) | collective-permute-done | bytes 2883616 | tf_op jit(solution)/shard_map/cond/branch_0_fun/ppermute | solution.py:405
  66.3 2.9 %merge.6 = (f32[12,64,256]{2,1,0:T(8,128)S(1)}, f32[12,64,256]{2,1,0:T(8,128)S(1)}, f32[12,64,256]{2,1,0:T(8,128)S(1)}, f32[12,64,256]{2,1,0:T(8,128)S(1)}, s32[1]{0:T(128)}) custom-call(s32[63,128]{1,0:T(8,128)S(1)} %copy-done.1, s32[1]{0:T(128)} %get-tuple-element.27.refs_1_, f32[22,128,256]{2,1,0:T(8,128)S(1)} %get-tuple-element.28.refs_2_, ...), custom_call_target="tpu_custom_call" | custom-call | flops 99999997952 | bytes 1 | tf_op jit(solution)/shard_map/cond/branch_0_fun/merge/pallas_call | solution.py:218
  71.7 18.5 %collective-permute-start.9 = (f32[12,64,256]{2,1,0:T(8,128)S(1)}, f32[12,64,256]{2,1,0:T(8,128)S(1)}, u32[]{:S(2)}, u32[]{:S(2)}) collective-permute-start(f32[12,64,256]{2,1,0:T(8,128)S(1)} %get-tuple-element.35), channel_id=1, source_target_pairs={{0,2},{1,3},{2,0},{3,1},{4,6},{5,7},{6,4},{7,5},{8,10},{9,11},{10,... | collective-permute-start | bytes 2359304 | tf_op jit(solution)/shard_map/cond/branch_0_fun/ppermute | solution.py:395
  90.7 13.5 %multiply.7 = (f32[22,128,256]{2,1,0:T(8,128)S(1)}, f32[22,128,256]{2,1,0:T(8,128)S(1)}, s32[1]{0:T(128)}) custom-call(s32[2]{0:T(128)S(1)} %copy-done.5, s32[3,64]{1,0:T(4,128)S(1)} %copy-done.15, s32[63,128]{1,0:T(8,128)S(1)} %copy-done.1, s32[1]{0:T(128)} %get-tuple-element.31.token_ref, f32[8192,1024]{1,0:T(8,128)} %get-tuple-element.185.inverse_ref, ...), custom_call_target="tpu_custom_call" | custom-call | flops 99999997952 | bytes 1 | tf_op jit(solution)/shard_map/cond/branch_0_fun/multiply/pallas_call | solution.py:190
  104.6 4.3 %collective-permute-done.10.refs_5_ = f32[12,64,256]{2,1,0:T(8,128)S(1)} collective-permute-done((f32[12,64,256]{2,1,0:T(8,128)S(1)}, f32[12,64,256]{2,1,0:T(8,128)S(1)}, u32[]{:S(2)}, u32[]{:S(2)}) %collective-permute-start.10) | collective-permute-done | bytes 786464 | tf_op jit(solution)/shard_map/cond/branch_0_fun/ppermute | solution.py:395
  108.9 2.9 %step.12 = (f32[7,64,256]{2,1,0:T(8,128)}, f32[7,64,256]{2,1,0:T(8,128)S(1)}, f32[7,64,256]{2,1,0:T(8,128)}, f32[7,64,256]{2,1,0:T(8,128)S(1)}, s32[1]{0:T(128)}) custom-call(s32[63,128]{1,0:T(8,128)S(1)} %copy-done.1, s32[1]{0:T(128)} %get-tuple-element.32.refs_1_, f32[12,64,256]{2,1,0:T(8,128)S(1)} %get-tuple-element.33.refs_2_, ...), custom_call_target="tpu_custom_call" | custom-call | flops 99999997952 | bytes 1 | tf_op jit(solution)/shard_map/cond/branch_0_fun/step/pallas_call | solution.py:218
  111.8 2.0 collective-permute-start.13
  113.8 1.7 collective-permute-start.14
  115.5 3.5 %merge.7 = (f32[12,64,256]{2,1,0:T(8,128)}, f32[12,64,256]{2,1,0:T(8,128)S(1)}, f32[12,64,256]{2,1,0:T(8,128)}, f32[12,64,256]{2,1,0:T(8,128)S(1)}, s32[1]{0:T(128)}) custom-call(s32[63,128]{1,0:T(8,128)S(1)} %copy-done.1, s32[1]{0:T(128)} %get-tuple-element.37.refs_1_, f32[22,128,256]{2,1,0:T(8,128)S(1)} %get-tuple-element.38.refs_2_, ...), custom_call_target="tpu_custom_call" | custom-call | flops 99999997952 | bytes 1 | tf_op jit(solution)/shard_map/cond/branch_0_fun/merge/pallas_call | solution.py:218
  119.6 13.5 %multiply.8 = (f32[22,128,256]{2,1,0:T(8,128)S(1)}, f32[22,128,256]{2,1,0:T(8,128)S(1)}, s32[1]{0:T(128)}) custom-call(s32[2]{0:T(128)S(1)} %copy-done.6, s32[3,64]{1,0:T(4,128)S(1)} %copy-done.16, s32[63,128]{1,0:T(8,128)S(1)} %copy-done.1, s32[1]{0:T(128)} %get-tuple-element.40.token_ref, f32[8192,1024]{1,0:T(8,128)} %get-tuple-element.185.inverse_ref, ...), custom_call_target="tpu_custom_call" | custom-call | flops 99999997952 | bytes 1 | tf_op jit(solution)/shard_map/cond/branch_0_fun/multiply/pallas_call | solution.py:190
  133.1 2.8 step.13
  135.9 2.4 collective-permute-start.18
  138.9 4.0 %collective-permute-done.15.refs_4_ = f32[12,64,256]{2,1,0:T(8,128)} collective-permute-done((f32[12,64,256]{2,1,0:T(8,128)}, f32[12,64,256]{2,1,0:T(8,128)}, u32[]{:S(2)}, u32[]{:S(2)}) %collective-permute-start.15) | collective-permute-done | bytes 786464 | tf_op jit(solution)/shard_map/cond/branch_0_fun/ppermute | solution.py:395
  142.9 2.1 collective-permute-done.16.refs_5_
  145.0 3.3 %step.14 = (f32[7,64,256]{2,1,0:T(8,128)}, f32[7,64,256]{2,1,0:T(8,128)S(1)}, f32[7,64,256]{2,1,0:T(8,128)}, f32[7,64,256]{2,1,0:T(8,128)S(1)}, s32[1]{0:T(128)}) custom-call(s32[63,128]{1,0:T(8,128)S(1)} %copy-done.1, s32[1]{0:T(128)} %get-tuple-element.47.refs_1_, f32[12,64,256]{2,1,0:T(8,128)S(1)} %get-tuple-element.48.refs_2_, ...), custom_call_target="tpu_custom_call" | custom-call | flops 99999997952 | bytes 1 | tf_op jit(solution)/shard_map/cond/branch_0_fun/step/pallas_call | solution.py:218
  149.4 3.5 %merge.8 = (f32[12,64,256]{2,1,0:T(8,128)}, f32[12,64,256]{2,1,0:T(8,128)S(1)}, f32[12,64,256]{2,1,0:T(8,128)}, f32[12,64,256]{2,1,0:T(8,128)S(1)}, s32[1]{0:T(128)}) custom-call(s32[63,128]{1,0:T(8,128)S(1)} %copy-done.1, s32[1]{0:T(128)} %get-tuple-element.52.refs_1_, f32[22,128,256]{2,1,0:T(8,128)S(1)} %get-tuple-element.53.refs_2_, ...), custom_call_target="tpu_custom_call" | custom-call | flops 99999997952 | bytes 1 | tf_op jit(solution)/shard_map/cond/branch_0_fun/merge/pallas_call | solution.py:218
  154.1 3.3 %collective-permute-done.18.refs_6_ = f32[4,64,256]{2,1,0:T(8,128)} collective-permute-done((f32[4,64,256]{2,1,0:T(8,128)}, f32[4,64,256]{2,1,0:T(8,128)}, u32[]{:S(2)}, u32[]{:S(2)}) %collective-permute-start.18) | collective-permute-done | bytes 262176 | tf_op jit(solution)/shard_map/cond/branch_0_fun/ppermute | solution.py:395
  157.4 3.9 %collective-permute-done.19.refs_7_ = f32[4,64,256]{2,1,0:T(8,128)} collective-permute-done((f32[4,64,256]{2,1,0:T(8,128)}, f32[4,64,256]{2,1,0:T(8,128)}, u32[]{:S(2)}, u32[]{:S(2)}) %collective-permute-start.19) | collective-permute-done | bytes 262176 | tf_op jit(solution)/shard_map/cond/branch_0_fun/ppermute | solution.py:395
  161.3 2.3 collect.6
  163.6 5.8 %collective-permute-done.20.refs_4_ = f32[7,64,256]{2,1,0:T(8,128)} collective-permute-done((f32[7,64,256]{2,1,0:T(8,128)}, f32[7,64,256]{2,1,0:T(8,128)}, u32[]{:S(2)}, u32[]{:S(2)}) %collective-permute-start.20) | collective-permute-done | bytes 458784 | tf_op jit(solution)/shard_map/cond/branch_0_fun/ppermute | solution.py:395
  169.4 2.5 step.15
  172.0 2.9 %collective-permute-start.25 = (f32[4,64,256]{2,1,0:T(8,128)S(1)}, f32[4,64,256]{2,1,0:T(8,128)S(1)}, u32[]{:S(2)}, u32[]{:S(2)}) collective-permute-start(f32[4,64,256]{2,1,0:T(8,128)S(1)} %get-tuple-element.74), channel_id=1, source_target_pairs={{0,8},{1,9},{2,10},{3,11},{4,12},{5,13},{6,14},{7,15},{8,0},{9,1},... | collective-permute-start | bytes 786440 | tf_op jit(solution)/shard_map/cond/branch_0_fun/ppermute | solution.py:395
  174.9 1.6 collective-permute-done.22.refs_4_
  176.5 18.8 %collective-permute-done.23.refs_5_ = f32[12,64,256]{2,1,0:T(8,128)} collective-permute-done((f32[12,64,256]{2,1,0:T(8,128)}, f32[12,64,256]{2,1,0:T(8,128)}, u32[]{:S(2)}, u32[]{:S(2)}) %collective-permute-start.23) | collective-permute-done | bytes 786464 | tf_op jit(solution)/shard_map/cond/branch_0_fun/ppermute | solution.py:395
  195.3 2.8 step.16
  198.2 2.1 collective-permute-start.27
  200.2 2.4 collect.7
  202.6 4.0 %collective-permute-done.26.refs_4_ = f32[7,64,256]{2,1,0:T(8,128)S(1)} collective-permute-done((f32[7,64,256]{2,1,0:T(8,128)S(1)}, f32[7,64,256]{2,1,0:T(8,128)S(1)}, u32[]{:S(2)}, u32[]{:S(2)}) %collective-permute-start.26) | collective-permute-done | bytes 458784 | tf_op jit(solution)/shard_map/cond/branch_0_fun/ppermute | solution.py:395
  206.7 2.3 step.17
  209.1 2.9 %collective-permute-start.29 = (f32[4,64,256]{2,1,0:T(8,128)S(1)}, f32[4,64,256]{2,1,0:T(8,128)S(1)}, u32[]{:S(2)}, u32[]{:S(2)}) collective-permute-start(f32[4,64,256]{2,1,0:T(8,128)S(1)} %get-tuple-element.84), channel_id=1, source_target_pairs={{0,8},{1,9},{2,10},{3,11},{4,12},{5,13},{6,14},{7,15},{8,0},{9,1},... | collective-permute-start | bytes 786440 | tf_op jit(solution)/shard_map/cond/branch_0_fun/ppermute | solution.py:395
  212.5 14.7 %collective-permute-done.28.refs_6_ = f32[4,64,256]{2,1,0:T(8,128)S(1)} collective-permute-done((f32[4,64,256]{2,1,0:T(8,128)S(1)}, f32[4,64,256]{2,1,0:T(8,128)S(1)}, u32[]{:S(2)}, u32[]{:S(2)}) %collective-permute-start.28) | collective-permute-done | bytes 262176 | tf_op jit(solution)/shard_map/cond/branch_0_fun/ppermute | solution.py:395
  227.3 3.5 %collective-permute-done.29.refs_7_ = f32[4,64,256]{2,1,0:T(8,128)S(1)} collective-permute-done((f32[4,64,256]{2,1,0:T(8,128)S(1)}, f32[4,64,256]{2,1,0:T(8,128)S(1)}, u32[]{:S(2)}, u32[]{:S(2)}) %collective-permute-start.29) | collective-permute-done | bytes 262176 | tf_op jit(solution)/shard_map/cond/branch_0_fun/ppermute | solution.py:395
  230.7 2.4 collect.8
  234.7 3.9 %finish.2 = (f32[512,768]{1,0:T(8,128)}, f32[768,256]{1,0:T(8,128)S(1)}, s32[1]{0:T(128)}) custom-call(s32[2]{0:T(128)S(1)} %copy-done.7, s32[1]{0:T(128)} %get-tuple-element.85.refs_1_, f32[512,768]{1,0:T(8,128)} %get-tuple-element.182.refs_2_, f32[2,128,256]{2,1,0:T(8,128)S(1)} %get-tuple-element.86.refs_3_, ...), custom_call_target="tpu_custom_call" | custom-call | flops 99999997952 | bytes 1 | tf_op jit(solution)/shard_map/cond/branch_0_fun/finish/pallas_call | solution.py:218
  240.7 2.0 collective-permute-start.36
  244.1 1.8 collective-permute-done.34
  245.9 2.0 collective-permute-done.36
  249.4 2.9 %collective-permute-start.39 = (f32[96,256]{1,0:T(8,128)S(1)}, f32[96,256]{1,0:T(8,128)S(1)}, u32[]{:S(2)}, u32[]{:S(2)}) collective-permute-start(f32[96,256]{1,0:T(8,128)S(1)} %add_add_fusion), channel_id=1, source_target_pairs={{0,12},{1,13},{2,14},{3,15},{4,8},{5,9},{6,10},{7,11},{8,4},{9,5},... | collective-permute-start | bytes 294920 | tf_op jit(solution)/shard_map/cond/branch_0_fun/ppermute | solution.py:315
  253.9 2.8 %collective-permute-done.39 = f32[96,256]{1,0:T(8,128)S(1)} collective-permute-done((f32[96,256]{1,0:T(8,128)S(1)}, f32[96,256]{1,0:T(8,128)S(1)}, u32[]{:S(2)}, u32[]{:S(2)}) %collective-permute-start.39) | collective-permute-done | bytes 98336 | tf_op jit(solution)/shard_map/cond/branch_0_fun/ppermute | solution.py:315
  256.7 3.2 %collective-permute-done.38 = f32[96,256]{1,0:T(8,128)S(1)} collective-permute-done((f32[96,256]{1,0:T(8,128)S(1)}, f32[96,256]{1,0:T(8,128)S(1)}, u32[]{:S(2)}, u32[]{:S(2)}) %collective-permute-start.38) | collective-permute-done | bytes 98336 | tf_op jit(solution)/shard_map/cond/branch_0_fun/ppermute | solution.py:315
  260.9 1.7 collective-permute-start.42
  264.4 2.7 collective-permute-done.42
  269.1 1.7 collective-permute-done.43
  (97 shorter events, 33.4 us)
Async XLA Ops:
  10.2 22.6 %copy-start.14 = (s32[3,64]{1,0:T(4,128)S(1)}, s32[3,64]{1,0:T(4,128)}, u32[]{:S(2)}) copy-start(s32[3,64]{1,0:T(4,128)} %get-tuple-element.24.fill_ref.refs_1_) | copy-start | bytes 2308 | tf_op jit(solution)/shard_map/cond
  11.7 1.4 collective-permute-start
  12.4 2.1 collective-permute-start.3
  13.1 2.9 %collective-permute-start.1 = (f32[512,256]{1,0:T(8,128)S(1)}, f32[512,256]{1,0:T(8,128)S(1)}, u32[]{:S(2)}, u32[]{:S(2)}) collective-permute-start(f32[512,256]{1,0:T(8,128)S(1)} %collective-permute-done), channel_id=1, source_target_pairs={{0,0},{1,8},{2,1},{3,9},{4,2},{5,10},{6,3},{7,11},{8,4},{9,12},{10... | collective-permute-start | bytes 1572872 | tf_op jit(solution)/shard_map/cond/branch_0_fun/ppermute | solution.py:377
  13.8 26.0 %collective-permute-start.5 = (f32[512,256]{1,0:T(8,128)S(1)}, f32[512,256]{1,0:T(8,128)S(1)}, u32[]{:S(2)}, u32[]{:S(2)}) collective-permute-start(f32[512,256]{1,0:T(8,128)S(1)} %get-tuple-element.203), channel_id=1, source_target_pairs={{0,0},{1,16},{2,2},{3,18},{4,4},{5,20},{6,6},{7,22},{8,8},{9,24},{... | collective-permute-start | bytes 1572872 | tf_op jit(solution)/shard_map/cond/branch_0_fun/ppermute | solution.py:365
  14.5 25.3 %collective-permute-start.4 = (f32[512,256]{1,0:T(8,128)S(1)}, f32[512,256]{1,0:T(8,128)}, u32[]{:S(2)}, u32[]{:S(2)}) collective-permute-start(f32[512,256]{1,0:T(8,128)S(1)} %collective-permute-done.3), channel_id=1, source_target_pairs={{0,0},{1,8},{2,1},{3,9},{4,2},{5,10},{6,3},{7,11},{8,4},{9,12},{10... | collective-permute-start | bytes 1572872 | tf_op jit(solution)/shard_map/cond/branch_0_fun/ppermute | solution.py:377
  16.0 30.7 %collective-permute-start.2 = (f32[512,256]{1,0:T(8,128)S(1)}, f32[512,256]{1,0:T(8,128)S(1)}, u32[]{:S(2)}, u32[]{:S(2)}) collective-permute-start(f32[512,256]{1,0:T(8,128)S(1)} %collective-permute-done.1.refs_0_), channel_id=1, source_target_pairs={{0,16},{16,0},{1,17},{17,1},{2,18},{18,2},{3,19},{19,3},{4,20},{20... | collective-permute-start | bytes 1572872 | tf_op jit(solution)/shard_map/cond/branch_0_fun/ppermute | solution.py:400
  48.0 18.3 %copy-start.1 = (s32[63,128]{1,0:T(8,128)S(1)}, s32[63,128]{1,0:T(8,128)}, u32[]{:S(2)}) copy-start(s32[63,128]{1,0:T(8,128)} %plan.2.table_ref.refs_0_.refs_2_) | copy-start | bytes 96772 | tf_op jit(solution)/shard_map/cond
  60.8 5.5 %collective-permute-start.6 = (f32[22,128,256]{2,1,0:T(8,128)S(1)}, f32[22,128,256]{2,1,0:T(8,128)S(1)}, u32[]{:S(2)}, u32[]{:S(2)}) collective-permute-start(f32[22,128,256]{2,1,0:T(8,128)S(1)} %get-tuple-element.29), channel_id=1, source_target_pairs={{0,1},{1,0},{2,3},{3,2},{4,5},{5,4},{6,7},{7,6},{8,9},{9,8},{10,11... | collective-permute-start | bytes 8650760 | tf_op jit(solution)/shard_map/cond/branch_0_fun/ppermute | solution.py:405
  61.4 7.8 %collective-permute-start.7 = (f32[512,256]{1,0:T(8,128)S(1)}, f32[512,256]{1,0:T(8,128)S(1)}, u32[]{:S(2)}, u32[]{:S(2)}) collective-permute-start(f32[512,256]{1,0:T(8,128)S(1)} %collective-permute-done.5.refs_3_), channel_id=1, source_target_pairs={{0,0},{1,8},{2,1},{3,9},{4,2},{5,10},{6,3},{7,11},{8,4},{9,12},{10... | collective-permute-start | bytes 1572872 | tf_op jit(solution)/shard_map/cond/branch_0_fun/ppermute | solution.py:377
  62.1 28.6 %collective-permute-start.8 = (f32[512,256]{1,0:T(8,128)}, f32[512,256]{1,0:T(8,128)}, u32[]{:S(2)}, u32[]{:S(2)}) collective-permute-start(f32[512,256]{1,0:T(8,128)} %collective-permute-done.4.refs_2_.refs_0_), channel_id=1, source_target_pairs={{0,16},{16,0},{1,17},{17,1},{2,18},{18,2},{3,19},{19,3},{4,20},{20... | collective-permute-start | bytes 1572872 | tf_op jit(solution)/shard_map/cond/branch_0_fun/ppermute | solution.py:400
  69.2 21.4 %copy-start.5 = (s32[2]{0:T(128)S(1)}, s32[2]{0:T(128)}, u32[]{:S(2)}) copy-start(s32[2]{0:T(128)} %pad_add_fusion.where_ref.refs_0_) | copy-start | bytes 28 | tf_op jit(solution)/shard_map/cond
  69.3 21.4 %copy-start.15 = (s32[3,64]{1,0:T(4,128)S(1)}, s32[3,64]{1,0:T(4,128)}, u32[]{:S(2)}) copy-start(s32[3,64]{1,0:T(4,128)} %get-tuple-element.24.fill_ref.refs_1_) | copy-start | bytes 2308 | tf_op jit(solution)/shard_map/cond
  70.8 48.8 %collective-permute-start.12 = (f32[512,256]{1,0:T(8,128)}, f32[512,256]{1,0:T(8,128)}, u32[]{:S(2)}, u32[]{:S(2)}) collective-permute-start(f32[512,256]{1,0:T(8,128)} %get-tuple-element.41.refs_0_), channel_id=1, source_target_pairs={{0,16},{16,0},{1,17},{17,1},{2,18},{18,2},{3,19},{19,3},{4,20},{20... | collective-permute-start | bytes 1572872 | tf_op jit(solution)/shard_map/cond/branch_0_fun/ppermute | solution.py:400
  71.7 32.8 %collective-permute-start.9 = (f32[12,64,256]{2,1,0:T(8,128)S(1)}, f32[12,64,256]{2,1,0:T(8,128)S(1)}, u32[]{:S(2)}, u32[]{:S(2)}) collective-permute-start(f32[12,64,256]{2,1,0:T(8,128)S(1)} %get-tuple-element.35), channel_id=1, source_target_pairs={{0,2},{1,3},{2,0},{3,1},{4,6},{5,7},{6,4},{7,5},{8,10},{9,11},{10,... | collective-permute-start | bytes 2359304 | tf_op jit(solution)/shard_map/cond/branch_0_fun/ppermute | solution.py:395
  90.2 18.7 %collective-permute-start.10 = (f32[12,64,256]{2,1,0:T(8,128)S(1)}, f32[12,64,256]{2,1,0:T(8,128)S(1)}, u32[]{:S(2)}, u32[]{:S(2)}) collective-permute-start(f32[12,64,256]{2,1,0:T(8,128)S(1)} %get-tuple-element.36), channel_id=1, source_target_pairs={{0,4},{1,5},{2,6},{3,7},{4,0},{5,1},{6,2},{7,3},{8,12},{9,13},{10,... | collective-permute-start | bytes 2359304 | tf_op jit(solution)/shard_map/cond/branch_0_fun/ppermute | solution.py:395
  104.2 11.3 %collective-permute-start.11 = (f32[22,128,256]{2,1,0:T(8,128)S(1)}, f32[22,128,256]{2,1,0:T(8,128)S(1)}, u32[]{:S(2)}, u32[]{:S(2)}) collective-permute-start(f32[22,128,256]{2,1,0:T(8,128)S(1)} %get-tuple-element.39), channel_id=1, source_target_pairs={{0,1},{1,0},{2,3},{3,2},{4,5},{5,4},{6,7},{7,6},{8,9},{9,8},{10,11... | collective-permute-start | bytes 8650760 | tf_op jit(solution)/shard_map/cond/branch_0_fun/ppermute | solution.py:405
  111.8 21.3 %collective-permute-start.13 = (f32[7,64,256]{2,1,0:T(8,128)}, f32[7,64,256]{2,1,0:T(8,128)}, u32[]{:S(2)}, u32[]{:S(2)}) collective-permute-start(f32[7,64,256]{2,1,0:T(8,128)} %get-tuple-element.45), channel_id=1, source_target_pairs={{0,4},{1,5},{2,6},{3,7},{4,0},{5,1},{6,2},{7,3},{8,12},{9,13},{10,... | collective-permute-start | bytes 1376264 | tf_op jit(solution)/shard_map/cond/branch_0_fun/ppermute | solution.py:395
  113.8 19.3 %collective-permute-start.14 = (f32[7,64,256]{2,1,0:T(8,128)}, f32[7,64,256]{2,1,0:T(8,128)}, u32[]{:S(2)}, u32[]{:S(2)}) collective-permute-start(f32[7,64,256]{2,1,0:T(8,128)} %get-tuple-element.46), channel_id=1, source_target_pairs={{0,2},{1,3},{2,0},{3,1},{4,6},{5,7},{6,4},{7,5},{8,10},{9,11},{10,... | collective-permute-start | bytes 1376264 | tf_op jit(solution)/shard_map/cond/branch_0_fun/ppermute | solution.py:395
  119.1 23.8 %collective-permute-start.15 = (f32[12,64,256]{2,1,0:T(8,128)}, f32[12,64,256]{2,1,0:T(8,128)}, u32[]{:S(2)}, u32[]{:S(2)}) collective-permute-start(f32[12,64,256]{2,1,0:T(8,128)} %get-tuple-element.50), channel_id=1, source_target_pairs={{0,2},{1,3},{2,0},{3,1},{4,6},{5,7},{6,4},{7,5},{8,10},{9,11},{10,... | collective-permute-start | bytes 2359304 | tf_op jit(solution)/shard_map/cond/branch_0_fun/ppermute | solution.py:395
  119.4 25.6 %collective-permute-start.16 = (f32[12,64,256]{2,1,0:T(8,128)}, f32[12,64,256]{2,1,0:T(8,128)}, u32[]{:S(2)}, u32[]{:S(2)}) collective-permute-start(f32[12,64,256]{2,1,0:T(8,128)} %get-tuple-element.51), channel_id=1, source_target_pairs={{0,4},{1,5},{2,6},{3,7},{4,0},{5,1},{6,2},{7,3},{8,12},{9,13},{10,... | collective-permute-start | bytes 2359304 | tf_op jit(solution)/shard_map/cond/branch_0_fun/ppermute | solution.py:395
  135.9 21.5 %collective-permute-start.18 = (f32[4,64,256]{2,1,0:T(8,128)}, f32[4,64,256]{2,1,0:T(8,128)}, u32[]{:S(2)}, u32[]{:S(2)}) collective-permute-start(f32[4,64,256]{2,1,0:T(8,128)} %get-tuple-element.58), channel_id=1, source_target_pairs={{0,8},{1,9},{2,10},{3,11},{4,12},{5,13},{6,14},{7,15},{8,0},{9,1},... | collective-permute-start | bytes 786440 | tf_op jit(solution)/shard_map/cond/branch_0_fun/ppermute | solution.py:395
  138.3 22.9 %collective-permute-start.19 = (f32[4,64,256]{2,1,0:T(8,128)}, f32[4,64,256]{2,1,0:T(8,128)}, u32[]{:S(2)}, u32[]{:S(2)}) collective-permute-start(f32[4,64,256]{2,1,0:T(8,128)} %get-tuple-element.59), channel_id=1, source_target_pairs={{0,8},{1,9},{2,10},{3,11},{4,12},{5,13},{6,14},{7,15},{8,0},{9,1},... | collective-permute-start | bytes 786440 | tf_op jit(solution)/shard_map/cond/branch_0_fun/ppermute | solution.py:395
  138.9 10.5 %collective-permute-start.17 = (f32[22,128,256]{2,1,0:T(8,128)S(1)}, f32[22,128,256]{2,1,0:T(8,128)S(1)}, u32[]{:S(2)}, u32[]{:S(2)}) collective-permute-start(f32[22,128,256]{2,1,0:T(8,128)S(1)} %get-tuple-element.54), channel_id=1, source_target_pairs={{0,1},{1,0},{2,3},{3,2},{4,5},{5,4},{6,7},{7,6},{8,9},{9,8},{10,11... | collective-permute-start | bytes 8650760 | tf_op jit(solution)/shard_map/cond/branch_0_fun/ppermute | solution.py:405
  148.3 21.1 %collective-permute-start.20 = (f32[7,64,256]{2,1,0:T(8,128)}, f32[7,64,256]{2,1,0:T(8,128)}, u32[]{:S(2)}, u32[]{:S(2)}) collective-permute-start(f32[7,64,256]{2,1,0:T(8,128)} %get-tuple-element.63), channel_id=1, source_target_pairs={{0,4},{1,5},{2,6},{3,7},{4,0},{5,1},{6,2},{7,3},{8,12},{9,13},{10,... | collective-permute-start | bytes 1376264 | tf_op jit(solution)/shard_map/cond/branch_0_fun/ppermute | solution.py:395
  148.4 21.0 %collective-permute-start.21 = (f32[7,64,256]{2,1,0:T(8,128)}, f32[7,64,256]{2,1,0:T(8,128)}, u32[]{:S(2)}, u32[]{:S(2)}) collective-permute-start(f32[7,64,256]{2,1,0:T(8,128)} %get-tuple-element.64), channel_id=1, source_target_pairs={{0,2},{1,3},{2,0},{3,1},{4,6},{5,7},{6,4},{7,5},{8,10},{9,11},{10,... | collective-permute-start | bytes 1376264 | tf_op jit(solution)/shard_map/cond/branch_0_fun/ppermute | solution.py:395
  152.9 23.6 %collective-permute-start.22 = (f32[12,64,256]{2,1,0:T(8,128)}, f32[12,64,256]{2,1,0:T(8,128)}, u32[]{:S(2)}, u32[]{:S(2)}) collective-permute-start(f32[12,64,256]{2,1,0:T(8,128)} %get-tuple-element.68), channel_id=1, source_target_pairs={{0,2},{1,3},{2,0},{3,1},{4,6},{5,7},{6,4},{7,5},{8,10},{9,11},{10,... | collective-permute-start | bytes 2359304 | tf_op jit(solution)/shard_map/cond/branch_0_fun/ppermute | solution.py:395
  157.4 37.9 %collective-permute-start.23 = (f32[12,64,256]{2,1,0:T(8,128)}, f32[12,64,256]{2,1,0:T(8,128)}, u32[]{:S(2)}, u32[]{:S(2)}) collective-permute-start(f32[12,64,256]{2,1,0:T(8,128)} %get-tuple-element.69), channel_id=1, source_target_pairs={{0,4},{1,5},{2,6},{3,7},{4,0},{5,1},{6,2},{7,3},{8,12},{9,13},{10,... | collective-permute-start | bytes 2359304 | tf_op jit(solution)/shard_map/cond/branch_0_fun/ppermute | solution.py:395
  171.9 28.3 %collective-permute-start.24 = (f32[4,64,256]{2,1,0:T(8,128)S(1)}, f32[4,64,256]{2,1,0:T(8,128)S(1)}, u32[]{:S(2)}, u32[]{:S(2)}) collective-permute-start(f32[4,64,256]{2,1,0:T(8,128)S(1)} %get-tuple-element.73), channel_id=1, source_target_pairs={{0,8},{1,9},{2,10},{3,11},{4,12},{5,13},{6,14},{7,15},{8,0},{9,1},... | collective-permute-start | bytes 786440 | tf_op jit(solution)/shard_map/cond/branch_0_fun/ppermute | solution.py:395
  172.0 28.3 %collective-permute-start.25 = (f32[4,64,256]{2,1,0:T(8,128)S(1)}, f32[4,64,256]{2,1,0:T(8,128)S(1)}, u32[]{:S(2)}, u32[]{:S(2)}) collective-permute-start(f32[4,64,256]{2,1,0:T(8,128)S(1)} %get-tuple-element.74), channel_id=1, source_target_pairs={{0,8},{1,9},{2,10},{3,11},{4,12},{5,13},{6,14},{7,15},{8,0},{9,1},... | collective-permute-start | bytes 786440 | tf_op jit(solution)/shard_map/cond/branch_0_fun/ppermute | solution.py:395
  198.1 8.5 %collective-permute-start.26 = (f32[7,64,256]{2,1,0:T(8,128)S(1)}, f32[7,64,256]{2,1,0:T(8,128)S(1)}, u32[]{:S(2)}, u32[]{:S(2)}) collective-permute-start(f32[7,64,256]{2,1,0:T(8,128)S(1)} %get-tuple-element.78), channel_id=1, source_target_pairs={{0,4},{1,5},{2,6},{3,7},{4,0},{5,1},{6,2},{7,3},{8,12},{9,13},{10,... | collective-permute-start | bytes 1376264 | tf_op jit(solution)/shard_map/cond/branch_0_fun/ppermute | solution.py:395
  198.2 8.5 %collective-permute-start.27 = (f32[7,64,256]{2,1,0:T(8,128)S(1)}, f32[7,64,256]{2,1,0:T(8,128)S(1)}, u32[]{:S(2)}, u32[]{:S(2)}) collective-permute-start(f32[7,64,256]{2,1,0:T(8,128)S(1)} %get-tuple-element.79), channel_id=1, source_target_pairs={{0,2},{1,3},{2,0},{3,1},{4,6},{5,7},{6,4},{7,5},{8,10},{9,11},{10,... | collective-permute-start | bytes 1376264 | tf_op jit(solution)/shard_map/cond/branch_0_fun/ppermute | solution.py:395
  209.0 18.2 %collective-permute-start.28 = (f32[4,64,256]{2,1,0:T(8,128)S(1)}, f32[4,64,256]{2,1,0:T(8,128)S(1)}, u32[]{:S(2)}, u32[]{:S(2)}) collective-permute-start(f32[4,64,256]{2,1,0:T(8,128)S(1)} %get-tuple-element.83), channel_id=1, source_target_pairs={{0,8},{1,9},{2,10},{3,11},{4,12},{5,13},{6,14},{7,15},{8,0},{9,1},... | collective-permute-start | bytes 786440 | tf_op jit(solution)/shard_map/cond/branch_0_fun/ppermute | solution.py:395
  209.1 21.6 %collective-permute-start.29 = (f32[4,64,256]{2,1,0:T(8,128)S(1)}, f32[4,64,256]{2,1,0:T(8,128)S(1)}, u32[]{:S(2)}, u32[]{:S(2)}) collective-permute-start(f32[4,64,256]{2,1,0:T(8,128)S(1)} %get-tuple-element.84), channel_id=1, source_target_pairs={{0,8},{1,9},{2,10},{3,11},{4,12},{5,13},{6,14},{7,15},{8,0},{9,1},... | collective-permute-start | bytes 786440 | tf_op jit(solution)/shard_map/cond/branch_0_fun/ppermute | solution.py:395
  212.0 21.2 %collective-permute-start.30 = (f32[2,128,256]{2,1,0:T(8,128)S(1)}, f32[2,128,256]{2,1,0:T(8,128)S(1)}, u32[]{:S(2)}, u32[]{:S(2)}) collective-permute-start(f32[2,128,256]{2,1,0:T(8,128)S(1)} %get-tuple-element.87), channel_id=1, source_target_pairs={{0,1},{1,0},{2,3},{3,2},{4,5},{5,4},{6,7},{7,6},{8,9},{9,8},{10,11... | collective-permute-start | bytes 786440 | tf_op jit(solution)/shard_map/cond/branch_0_fun/ppermute | solution.py:425
  212.0 21.2 %collective-permute-start.31 = (f32[2,128,256]{2,1,0:T(8,128)S(1)}, f32[2,128,256]{2,1,0:T(8,128)S(1)}, u32[]{:S(2)}, u32[]{:S(2)}) collective-permute-start(f32[2,128,256]{2,1,0:T(8,128)S(1)} %get-tuple-element.89), channel_id=1, source_target_pairs={{0,1},{1,0},{2,3},{3,2},{4,5},{5,4},{6,7},{7,6},{8,9},{9,8},{10,11... | collective-permute-start | bytes 786440 | tf_op jit(solution)/shard_map/cond/branch_0_fun/ppermute | solution.py:425
  233.1 1.6 collective-permute-start.32
  238.7 1.8 collective-permute-start.33
  240.6 5.3 %collective-permute-start.34 = (f32[96,256]{1,0:T(8,128)S(1)}, f32[96,256]{1,0:T(8,128)S(1)}, u32[]{:S(2)}, u32[]{:S(2)}) collective-permute-start(f32[96,256]{1,0:T(8,128)S(1)} %get-tuple-element.214), channel_id=1, source_target_pairs={{0,2},{1,3},{2,0},{3,1},{4,6},{5,7},{6,4},{7,5},{8,10},{9,11},{10,... | collective-permute-start | bytes 294920 | tf_op jit(solution)/shard_map/cond/branch_0_fun/ppermute | solution.py:315
  240.7 7.3 %collective-permute-start.36 = (f32[96,256]{1,0:T(8,128)S(1)}, f32[96,256]{1,0:T(8,128)S(1)}, u32[]{:S(2)}, u32[]{:S(2)}) collective-permute-start(f32[96,256]{1,0:T(8,128)S(1)} %get-tuple-element.215), channel_id=1, source_target_pairs={{0,18},{1,19},{2,16},{3,17},{4,22},{5,23},{6,20},{7,21},{8,26},{9,... | collective-permute-start | bytes 294920 | tf_op jit(solution)/shard_map/cond/branch_0_fun/ppermute | solution.py:315
  242.7 6.7 %collective-permute-start.35 = (f32[96,256]{1,0:T(8,128)S(1)}, f32[96,256]{1,0:T(8,128)S(1)}, u32[]{:S(2)}, u32[]{:S(2)}) collective-permute-start(f32[96,256]{1,0:T(8,128)S(1)} %get-tuple-element.216), channel_id=1, source_target_pairs={{0,16},{1,17},{2,18},{3,19},{4,20},{5,21},{6,22},{7,23},{8,24},{9,... | collective-permute-start | bytes 294920 | tf_op jit(solution)/shard_map/cond/branch_0_fun/ppermute | solution.py:315
  249.4 7.3 %collective-permute-start.39 = (f32[96,256]{1,0:T(8,128)S(1)}, f32[96,256]{1,0:T(8,128)S(1)}, u32[]{:S(2)}, u32[]{:S(2)}) collective-permute-start(f32[96,256]{1,0:T(8,128)S(1)} %add_add_fusion), channel_id=1, source_target_pairs={{0,12},{1,13},{2,14},{3,15},{4,8},{5,9},{6,10},{7,11},{8,4},{9,5},... | collective-permute-start | bytes 294920 | tf_op jit(solution)/shard_map/cond/branch_0_fun/ppermute | solution.py:315
  252.3 7.6 %collective-permute-start.38 = (f32[96,256]{1,0:T(8,128)S(1)}, f32[96,256]{1,0:T(8,128)S(1)}, u32[]{:S(2)}, u32[]{:S(2)}) collective-permute-start(f32[96,256]{1,0:T(8,128)S(1)} %add_add_fusion), channel_id=1, source_target_pairs={{0,8},{1,9},{2,10},{3,11},{4,12},{5,13},{6,14},{7,15},{8,0},{9,1},... | collective-permute-start | bytes 294920 | tf_op jit(solution)/shard_map/cond/branch_0_fun/ppermute | solution.py:315
  252.3 7.6 %collective-permute-start.37 = (f32[96,256]{1,0:T(8,128)S(1)}, f32[96,256]{1,0:T(8,128)S(1)}, u32[]{:S(2)}, u32[]{:S(2)}) collective-permute-start(f32[96,256]{1,0:T(8,128)S(1)} %add_add_fusion), channel_id=1, source_target_pairs={{0,4},{1,5},{2,6},{3,7},{4,0},{5,1},{6,2},{7,3},{8,12},{9,13},{10,... | collective-permute-start | bytes 294920 | tf_op jit(solution)/shard_map/cond/branch_0_fun/ppermute | solution.py:315
  260.9 6.3 %collective-permute-start.42 = (f32[96,256]{1,0:T(8,128)S(1)}, f32[96,256]{1,0:T(8,128)S(1)}, u32[]{:S(2)}, u32[]{:S(2)}) collective-permute-start(f32[96,256]{1,0:T(8,128)S(1)} %bitcast_subtract_fusion), channel_id=1, source_target_pairs={{0,18},{1,19},{2,16},{3,17},{4,22},{5,23},{6,20},{7,21},{8,26},{9,... | collective-permute-start | bytes 294920 | tf_op jit(solution)/shard_map/cond/branch_0_fun/ppermute | solution.py:315
  262.6 6.1 %collective-permute-start.41 = (f32[96,256]{1,0:T(8,128)S(1)}, f32[96,256]{1,0:T(8,128)S(1)}, u32[]{:S(2)}, u32[]{:S(2)}) collective-permute-start(f32[96,256]{1,0:T(8,128)S(1)} %bitcast_subtract_fusion), channel_id=1, source_target_pairs={{0,16},{1,17},{2,18},{3,19},{4,20},{5,21},{6,22},{7,23},{8,24},{9,... | collective-permute-start | bytes 294920 | tf_op jit(solution)/shard_map/cond/branch_0_fun/ppermute | solution.py:315
  263.8 5.0 %collective-permute-start.40 = (f32[96,256]{1,0:T(8,128)S(1)}, f32[96,256]{1,0:T(8,128)S(1)}, u32[]{:S(2)}, u32[]{:S(2)}) collective-permute-start(f32[96,256]{1,0:T(8,128)S(1)} %bitcast_subtract_fusion), channel_id=1, source_target_pairs={{0,2},{1,3},{2,0},{3,1},{4,6},{5,7},{6,4},{7,5},{8,10},{9,11},{10,... | collective-permute-start | bytes 294920 | tf_op jit(solution)/shard_map/cond/branch_0_fun/ppermute | solution.py:315
  269.0 1.8 collective-permute-start.43
  (7 other events, 30.3 us)
